TPU v7x, 128 devices: a whole 4x4x4 slice. The times are simulated.
128 devices in a mesh: slit: 16 (over x, y_hi, core), span: 8 (over z, y_lo).
Axes of the slice: x: 4, y: 4 (y_hi: 2, y_lo: 2; y = y_hi * 2 + y_lo), z: 4, core: 2. Of those that a mesh axis runs over, the one named last changes fastest.
Arguments:
- query_tiles: bfloat16 [64, 16, 128, 768], P('slit', 'span'), may hold values from -4 to 4
- key_tiles: bfloat16 [64, 16, 128, 768], P('slit', 'span'), may hold values from -4 to 4
- value_tiles: bfloat16 [64, 16, 128, 768], P('slit', 'span'), may hold values from -3 to 3
- forward_out: bfloat16 [64, 16, 128, 768], P('slit', 'span'), may hold values from -3 to 3
- out_grad: bfloat16 [64, 16, 128, 768], P('slit', 'span'), may hold values from -3 to 3
- row_lse: float32 [64, 16, 12, 128], P('slit', 'span'), may hold values from 2 to 3.5
- neighbours: int32 [64, 16, 8], P('slit', 'span'), may hold values from 0 to 1023, as said below
- flags: int32 [64, 16, 8], P('slit', 'span'), may hold values from 0 to 1
Outputs:
- query_grad: bfloat16 [64, 16, 128, 768], P('slit', 'span')
- key_grad: bfloat16 [64, 16, 128, 768], P('slit', 'span')
- value_grad: bfloat16 [64, 16, 128, 768], P('slit', 'span')
Inputs may be any that keep to these rules, and one draw needn't show every extreme that they name: `neighbours`: every listed key block lies within one block of its query block along both directions (slit positions taken modulo 64, transverse positions not wrapped); the entries with flag 1 come first in each list, are distinct, number at least 1, and some query block has all 8 entries used; padded entries hold the query block's own id.
All inputs are finite; a program needn't handle non-finite values.
Results may differ from a plain program's by a relative error of at most 0.006.
Values may be sent and summed in bfloat16 or wider, within the bound.
No kernel may reach another device: no remote copies, remote signals or barrier semaphores. Data moves between devices by JAX's collectives and lax.ppermute only.
A program may use at most 192 MiB of HBM per device.

v0:
```python
import functools

import jax
import jax.numpy as jnp
from jax import lax
from jax.experimental import pallas as pl
from jax.experimental.pallas import tpu as pltpu
from jax.sharding import PartitionSpec as P

SUB = 2
BLK = 128
PAIR = 128
HALF = 64
PAIRS = 6
FIRST = 4
PAY = 2 * BLK + 16
FAR = 1.0e4
SCALE = 0.125
AXES = ("slit", "span")
VMEM = 64 * 1024 * 1024 - 128 * 1024
GRID_A = 64
GRID_B = 16

NT = (((1,), (1,)), ((), ()))
NN = (((1,), (0,)), ((), ()))


def dot(a, b, dims):
    return lax.dot_general(a, b, dims, preferred_element_type=jnp.float32)


def cat(xs, axis):
    return jnp.concatenate(xs, axis=axis) if len(xs) > 1 else xs[0]


def head_masks():
    lane = lax.broadcasted_iota(jnp.int32, (1, PAIR), 1)
    first = jnp.where(lane < HALF, 1.0, 0.0)
    return first.astype(jnp.bfloat16), (1.0 - first).astype(jnp.bfloat16)


def split_heads(x, masks):
    return jnp.concatenate([x * masks[0], x * masks[1]], axis=0)


def offset_row(dr, dc):
    o = (dr + 1) * 3 + dc + 1
    return 8 if o == 4 else (o if o < 4 else o - 1)


def twice(x):
    return jnp.concatenate([x, x], axis=1)


def attend(tasks, masks):
    scored = []
    for (q, do, _, _, _), keys, values, _ in tasks:
        q2 = split_heads(q * jnp.asarray(SCALE, jnp.bfloat16), masks)
        do2 = split_heads(do, masks)
        scored.append((q2, do2, dot(cat(keys, 0), q2, NT), dot(cat(values, 0), do2, NT)))
    weighted = []
    for ((_, _, lse, delta, biases), _, _, _), (_, _, s, dp) in zip(tasks, scored):
        p_parts, g_parts = [], []
        for n, bias in enumerate(biases):
            part = slice(n * BLK, (n + 1) * BLK)
            p = jnp.exp(s[part] - (lse + bias))
            p_parts.append(p.astype(jnp.bfloat16))
            g_parts.append((p * (dp[part] - delta)).astype(jnp.bfloat16))
        weighted.append((cat(p_parts, 0), cat(g_parts, 0)))
    results = []
    for (_, _, _, keys_t), (q2, do2, _, _), (p, g) in zip(tasks, scored, weighted):
        kt = cat(keys_t, 1)
        dv = dot(p, do2, NN)
        dk = dot(g, q2, NN)
        dq_t = jnp.concatenate(
            [dot(kt[:HALF], g[:, :BLK], NN), dot(kt[HALF:], g[:, BLK:], NN)], axis=0
        )
        results.append((dk, dv, dq_t))
    return results


def flip(block):
    return block.astype(jnp.float32).T.astype(jnp.bfloat16)


def by_rows(par, run, together=False):
    middle = [(1, [0, 1, 2]), (2, [1, 2, 3])]
    if not together:
        run(middle)

    for core, ends in enumerate(([(0, [0, 1]), (3, [2, 3, 4])], [(0, [-1, 0, 1]), (3, [2, 3])])):
        pl.when(par == core)(functools.partial(run, middle + ends if together else ends))


def row_sums(do, o):
    prod = do.astype(jnp.float32) * o.astype(jnp.float32)
    high = prod.astype(jnp.bfloat16)
    low = (prod - high.astype(jnp.float32)).astype(jnp.bfloat16)
    shape = (16, do.shape[1])
    row = lax.broadcasted_iota(jnp.int32, shape, 0)
    lane = lax.broadcasted_iota(jnp.int32, shape, 1)
    pick = jnp.where(row == lane // HALF, 1.0, 0.0).astype(jnp.bfloat16)
    return dot(pick, high, NT) + dot(pick, low, NT)


def mark_lists(pos_ref, near_ref, flag_ref, r, c, dst_ref, at):
    dst_ref[at] = jnp.zeros((16, BLK), jnp.float32)
    for e in range(8):
        key = near_ref[r, c, e]
        flag = flag_ref[r, c, e]
        da = key // GRID_B - (pos_ref[1] + r)
        da = jnp.where(da > 1, da - GRID_A, jnp.where(da < -1, da + GRID_A, da))
        db = key % GRID_B - (pos_ref[2] + c)
        o = (da + 1) * 3 + db + 1
        row = jnp.where(o == 4, 8, jnp.where(o > 4, o - 1, o))
        row = jnp.clip(jnp.where(flag != 0, row, 15), 0, 15)
        dst_ref[at + (pl.ds(row, 1),)] = jnp.ones((1, BLK), jnp.float32)


def fill_aux(aux_ref, lse, delta, used):
    for n in range(PAIRS):
        lanes = slice(n * BLK, (n + 1) * BLK)
        heads = slice(2 * n, 2 * n + 2)
        for start, x in ((0, lse[heads]), (4, delta[heads])):
            high = x.astype(jnp.bfloat16).astype(jnp.float32)
            aux_ref[start : start + 2, lanes] = high
            aux_ref[start + 2 : start + 4, lanes] = x - high
        aux_ref[8:16, lanes] = used


def prepare_column_kernel(pos_ref, near_ref, flag_ref, q_ref, do_ref, o_ref, lse_ref, delta_ref, used_ref, *rest, c):
    *col_refs, aux_ref = rest
    delta = row_sums(do_ref[0, 0], o_ref[0, 0])[0 : 2 * PAIRS]
    mark_lists(pos_ref, near_ref, flag_ref, pl.program_id(0), c, used_ref, (0,))
    fill_aux(aux_ref, lse_ref[0, c], delta, used_ref[0, 0:8])
    delta_ref[0] = delta
    start = 0
    for col_ref in col_refs:
        lanes = slice(start, start + col_ref.shape[2])
        start = lanes.stop
        col_ref[0, 0:BLK] = q_ref[0, 0, :, lanes]
        col_ref[0, BLK : 2 * BLK] = do_ref[0, 0, :, lanes]
        col_ref[0, 2 * BLK : PAY] = aux_ref[:, lanes].astype(jnp.bfloat16)


def prepare_row_kernel(pos_ref, near_ref, flag_ref, q_ref, do_ref, o_ref, lse_ref, out_ref, dg0_ref, dg1_ref, used_ref, aux_ref):
    delta = row_sums(do_ref[...].reshape(2 * BLK, FULL), o_ref[...].reshape(2 * BLK, FULL))
    for c, dg_ref in ((0, dg0_ref), (1, dg1_ref)):
        mark_lists(pos_ref, near_ref, flag_ref, 3 * pos_ref[0], c, used_ref, (c,))
        fill_aux(aux_ref.at[c], lse_ref[0, c], delta[0 : 2 * PAIRS, c * BLK : (c + 1) * BLK], used_ref[c, 0:8])
        for dst, at in ((out_ref, c), (dg_ref, 0)):
            dst[at, 0:BLK] = q_ref[0, c]
            dst[at, BLK : 2 * BLK] = do_ref[0, c]
            dst[at, 2 * BLK : PAY] = aux_ref[c].astype(jnp.bfloat16)


def local_kernel(pos_ref, q_ref, do_ref, k_ref, v_ref, ks_ref, lse_ref, delta0_ref, delta1_ref, used0_ref, used1_ref, dk_ref, dv_ref, sk_ref, sv_ref, dq_ref, kt_ref):
    h = pl.program_id(0)
    masks = head_masks()
    for c in range(2):
        lanes = slice(c * BLK, (c + 1) * BLK)
        for r in range(4):
            kt_ref[r, :, lanes] = flip(k_ref[r, c])
        kt_ref[4, :, lanes] = flip(ks_ref[0, c])
    for ref in (dk_ref, dv_ref, sk_ref, sv_ref):
        ref[...] = jnp.zeros_like(ref)

    def one(row, key_rows):
        tasks = []
        for c, delta_ref, used_ref in ((0, delta0_ref, used0_ref), (1, delta1_ref, used1_ref)):
            lse = [lse_ref[row, c, pl.ds(2 * h + i, 1), :] for i in range(2)]
            delta = [delta_ref[row, pl.ds(2 * h + i, 1), :] for i in range(2)]
            keys, values, keys_t, biases = [], [], [], []
            for r in key_rows:
                for kc in range(2):
                    sibling = r in (-1, 4)
                    keys.append(ks_ref[0, kc] if sibling else k_ref[r, kc])
                    values.append(ks_ref[1, kc] if sibling else v_ref[r, kc])
                    keys_t.append(kt_ref[4 if sibling else r, :, kc * BLK : (kc + 1) * BLK])
                    at = offset_row(r - row, kc - c)
                    biases.append(twice((1.0 - used_ref[row, at : at + 1, :]) * FAR))
            query = (q_ref[row, c], do_ref[row, c], cat(lse, 1), cat(delta, 1), biases)
            tasks.append((query, keys, values, keys_t))
        results = attend(tasks, masks)
        dk = results[0][0] + results[1][0]
        dv = results[0][1] + results[1][1]
        for n, r in enumerate(key_rows):
            for kc in range(2):
                part = slice((2 * n + kc) * BLK, (2 * n + kc + 1) * BLK)
                if r in (-1, 4):
                    sk_ref[kc] += dk[part]
                    sv_ref[kc] += dv[part]
                else:
                    dk_ref[r, kc] += dk[part]
                    dv_ref[r, kc] += dv[part]
        for c in range(2):
            dq_ref[row, c] = results[c][2].T * SCALE

    def run(groups):
        for row, key_rows in groups:
            one(row, key_rows)

    by_rows(pos_ref[0], run)


def received(ref, at, lanes, aux, rows):
    lse = aux[0:2] + aux[2:4]
    delta = aux[4:6] + aux[6:8]
    biases = [twice((1.0 - row) * FAR) for row in rows]
    stats = [cat([x[0:1], x[1:2]], 1) for x in (lse, delta)]
    return (ref[at, 0:BLK, lanes], ref[at, BLK : 2 * BLK, lanes], stats[0], stats[1], biases)


def column_kernel(pos_ref, k_ref, v_ref, ks_ref, col_ref, dkp_ref, dvp_ref, skp_ref, svp_ref, *rest, side, sub):
    dk_ref, dv_ref, sib_ref, tail_ref, res_ref, kt_ref, acck_ref, accv_ref, accs_ref = rest[-9:]
    masks = head_masks()
    for n in range(sub):
        lanes = slice(n * PAIR, (n + 1) * PAIR)
        for r in range(4):
            kt_ref[n, :, r * BLK : (r + 1) * BLK] = flip(k_ref[r, 0, :, lanes])
        kt_ref[n, :, 4 * BLK :] = flip(ks_ref[0, 0, :, lanes])
    acck_ref[...] = dkp_ref[:, 0]
    accv_ref[...] = dvp_ref[:, 0]
    accs_ref[0] = skp_ref[0]
    accs_ref[1] = svp_ref[0]

    def run(groups):
        tasks, places = [], []
        for n in range(sub):
            lanes = slice(n * PAIR, (n + 1) * PAIR)
            for row, key_rows in groups:
                aux = col_ref[row, 2 * BLK : PAY, lanes].astype(jnp.float32)
                keys, values, keys_t, rows = [], [], [], []
                for r in key_rows:
                    sibling = r in (-1, 4)
                    keys.append(ks_ref[0, 0, :, lanes] if sibling else k_ref[r, 0, :, lanes])
                    values.append(ks_ref[1, 0, :, lanes] if sibling else v_ref[r, 0, :, lanes])
                    at = 4 * BLK if sibling else r * BLK
                    keys_t.append(kt_ref[n, :, at : at + BLK])
                    at = 8 + offset_row(r - row, 1 - 2 * side)
                    rows.append(aux[at : at + 1])
                tasks.append((received(col_ref, row, lanes, aux, rows), keys, values, keys_t))
                places.append((row, key_rows, lanes))
        for (row, key_rows, lanes), (dk, dv, dq_t) in zip(places, attend(tasks, masks)):
            for n, r in enumerate(key_rows):
                part = slice(n * BLK, (n + 1) * BLK)
                if r in (-1, 4):
                    accs_ref[0, :, lanes] += dk[part]
                    accs_ref[1, :, lanes] += dv[part]
                else:
                    acck_ref[r, :, lanes] += dk[part]
                    accv_ref[r, :, lanes] += dv[part]
            res_ref[row, :, lanes] = (dq_t.T * SCALE).astype(jnp.bfloat16)

    by_rows(pos_ref[0], run, together=True)
    for r in range(4):
        dk_ref[r, 0] = acck_ref[r].astype(jnp.bfloat16)
        dv_ref[r, 0] = accv_ref[r].astype(jnp.bfloat16)
    sib_ref[0] = accs_ref[...].astype(jnp.bfloat16)
    for i in range(2):
        tail_ref[i, 0, 0] = acck_ref[3 * i]
        tail_ref[i, 0, 1] = accv_ref[3 * i]


def outer_kernel(pos_ref, k_ref, v_ref, out_ref, dg0_ref, dg1_ref, part_ref, ro_ref, rg0_ref, rg1_ref):
    masks = head_masks()
    below = pos_ref[0] == 0
    slots = ((dg0_ref, 0, rg0_ref, -1), (out_ref, 0, ro_ref, 0), (out_ref, 1, ro_ref, 1), (dg1_ref, 0, rg1_ref, 2))
    tasks, places = [], []
    for n in range(SUB):
        lanes = slice(n * PAIR, (n + 1) * PAIR)
        kts = [flip(k_ref[0, c, :, lanes]) for c in range(2)]
        for ref, at, res_ref, c in slots:
            near = [kc for kc in range(2) if abs(kc - c) <= 1]
            aux = ref[at, 2 * BLK : PAY, lanes].astype(jnp.float32)
            ups = [8 + kc - c + 1 for kc in near]
            rows = [jnp.where(below, aux[u + 5 : u + 6], aux[u : u + 1]) for u in ups]
            query = received(ref, at, lanes, aux, rows)
            keys = [k_ref[0, kc, :, lanes] for kc in near]
            values = [v_ref[0, kc, :, lanes] for kc in near]
            tasks.append((query, keys, values, [kts[kc] for kc in near]))
            places.append((lanes, at, res_ref, near))
    totals = {}
    for (lanes, at, res_ref, near), (dk, dv, dq_t) in zip(places, attend(tasks, masks)):
        for n, kc in enumerate(near):
            for i, x in enumerate((dk, dv)):
                x = x[n * BLK : (n + 1) * BLK]
                key = (kc, i, lanes.start)
                totals[key] = totals[key] + x if key in totals else x
        res_ref[at, :, lanes] = (dq_t.T * SCALE).astype(jnp.bfloat16)
    for (kc, i, start), x in totals.items():
        part_ref[kc, i, :, start : start + PAIR] = x


def queries_kernel(pos_ref, dq_ref, back_ref, row_ref, corner_ref, *rest):
    res_ref = rest[-1]
    for r in range(2):
        total = dq_ref[r, 0] + back_ref[r].astype(jnp.float32)
        edge = row_ref[0].astype(jnp.float32) + corner_ref[0].astype(jnp.float32)
        outer = 2 * pl.program_id(0) + r == 3 * pos_ref[0]
        res_ref[r, 0] = jnp.where(outer, total + edge, total).astype(jnp.bfloat16)


def edges_kernel(pos_ref, tail_ref, part_ref, sib_ref, dk_in, dv_in, dk_ref, dv_ref):
    outer = pl.program_id(0) == pos_ref[0]
    for c in range(2):
        for i, ref in enumerate((dk_ref, dv_ref)):
            add = jnp.where(outer, part_ref[c, i], sib_ref[c, i].astype(jnp.float32))
            ref[0, c] = (tail_ref[0, c, i] + add).astype(jnp.bfloat16)


def lanes_spec(shape, base=0, at=None):
    at = at or (0,) * (len(shape) - 1)
    return pl.BlockSpec(shape, lambda h, *_: at + (h + base,))


def rows_spec(shape, lane=0):
    return pl.BlockSpec(shape, lambda r, *_: (r,) + (0,) * (len(shape) - 2) + (lane,))


def fixed(shape, lane=0):
    return pl.BlockSpec(shape, lambda *_: (0,) * (len(shape) - 1) + (lane,))


SMEM = pl.BlockSpec(memory_space=pltpu.SMEM)
ANY = pl.BlockSpec(memory_space=pl.ANY)
TILES = (4, 2, BLK, PAIR)
FULL = PAIRS * PAIR


def sds(shape, dtype=jnp.bfloat16):
    return jax.ShapeDtypeStruct(shape, dtype)


def f32s(shape):
    return sds(shape, jnp.float32)


def call(kernel, name, grid, ins, outs, shapes, scratch=(), alias=None):
    return pl.pallas_call(
        kernel,
        grid_spec=pltpu.PrefetchScalarGridSpec(
            num_scalar_prefetch=1, grid=(grid,), in_specs=ins, out_specs=outs, scratch_shapes=scratch
        ),
        out_shape=shapes,
        input_output_aliases=alias or {},
        compiler_params=pltpu.CompilerParams(
            vmem_limit_bytes=VMEM, dimension_semantics=("arbitrary",)
        ),
        cost_estimate=pl.CostEstimate(flops=1, bytes_accessed=1, transcendentals=0),
        name=name,
    )


def prepare_column(pos, lists, q, do, o, lse, c, parts):
    block = pl.BlockSpec((1, 1, BLK, FULL), lambda r, _: (r, c, 0, 0))
    shapes = [(2 * PAIRS, BLK), (16, BLK)] + [(PAY, n * PAIR) for n in parts]
    kinds = [jnp.float32, jnp.float32] + [jnp.bfloat16] * len(parts)
    return call(
        functools.partial(prepare_column_kernel, c=c),
        "prepare_column",
        4,
        [SMEM] * 2 + [block] * 3 + [rows_spec((1, 2, 2 * PAIRS, BLK))],
        [rows_spec((1,) + shape) for shape in shapes],
        [sds((4,) + shape, kind) for shape, kind in zip(shapes, kinds)],
        [pltpu.VMEM((16, FULL), jnp.float32)],
    )(pos, *lists, q, do, o, lse)


def prepare_row(pos, lists, q, do, o, lse):
    outer = lambda shape: pl.BlockSpec(shape, lambda _, p: (3 * p[0], 0, 0, 0))
    shapes = [(2, PAY, FULL), (1, PAY, FULL), (1, PAY, FULL)]
    return call(
        prepare_row_kernel,
        "prepare_row",
        1,
        [SMEM] * 2 + [outer((1, 2, BLK, FULL))] * 3 + [outer((1, 2, 2 * PAIRS, BLK))],
        [fixed(shape) for shape in shapes],
        [sds(shape) for shape in shapes],
        [pltpu.VMEM((2, 16, BLK), jnp.float32), pltpu.VMEM((2, 16, FULL), jnp.float32)],
    )(pos, *lists, q, do, o, lse)


def local(pos, q, do, k, v, ks, lse, deltas, used):
    tiles = f32s((4, 2, BLK, FULL))
    edge = f32s((2, BLK, FULL))
    return call(
        local_kernel,
        "local",
        PAIRS,
        [lanes_spec(TILES)] * 4
        + [lanes_spec((2, 2, BLK, PAIR)), fixed((4, 2, 2 * PAIRS, BLK))]
        + [fixed((4, 2 * PAIRS, BLK))] * 2
        + [fixed((4, 16, BLK))] * 2,
        [lanes_spec(TILES)] * 2 + [lanes_spec((2, BLK, PAIR))] * 2 + [lanes_spec(TILES)],
        [tiles, tiles, edge, edge, tiles],
        [pltpu.VMEM((5, PAIR, 2 * BLK), jnp.bfloat16)],
    )(pos, q, do, k, v, ks, lse, *deltas, *used)


def column(pos, k, v, ks, col, parts, done, base, count, side):
    sub = SUB if count % SUB == 0 else 1
    wide = sub * PAIR
    at = base // sub
    column_of = lanes_spec((4, 1, BLK, wide), at, (0, side, 0))
    return call(
        functools.partial(column_kernel, side=side, sub=sub),
        "column",
        count // sub,
        [column_of] * 2
        + [lanes_spec((2, 1, BLK, wide), at, (0, side, 0)), lanes_spec((4, PAY, wide))]
        + [column_of] * 2
        + [lanes_spec((1, BLK, wide), at, (side, 0))] * 2
        + [ANY] * len(done),
        [column_of] * 2
        + [
            lanes_spec((1, 2, BLK, wide), at, (side, 0, 0)),
            lanes_spec((2, 1, 2, BLK, wide), at, (0, side, 0, 0)),
            lanes_spec((4, BLK, wide)),
        ],
        [sds((4, 2, BLK, FULL))] * 2
        + [sds((2, 2, BLK, FULL)), f32s((2, 2, 2, BLK, FULL)), sds((4, BLK, count * PAIR))],
        [pltpu.VMEM((sub, PAIR, 5 * BLK), jnp.bfloat16)]
        + [pltpu.VMEM((4, BLK, wide), jnp.float32)] * 2
        + [pltpu.VMEM((2, BLK, wide), jnp.float32)],
        alias={9 + i: i for i in range(len(done))},
    )(pos, k, v, ks, col, *parts, *done)


def outers(pos, k, v, out, dg0, dg1):
    sizes = (2, 1, 1)
    wide = SUB * PAIR
    outer = pl.BlockSpec((1, 2, BLK, wide), lambda h, p: (3 * p[0], 0, 0, h))
    return call(
        outer_kernel,
        "outer_rows",
        PAIRS // SUB,
        [outer] * 2 + [lanes_spec((n, PAY, wide)) for n in sizes],
        [lanes_spec((2, 2, BLK, wide))] + [lanes_spec((n, BLK, wide)) for n in sizes],
        [f32s((2, 2, BLK, FULL))] + [sds((n, BLK, FULL)) for n in sizes],
    )(pos, k, v, out, dg0, dg1)


def finish_queries(pos, dqp, back, back_out, corner, done, c, base, count):
    wide = count * PAIR
    lane = base // count
    block = pl.BlockSpec((2, 1, BLK, wide), lambda r, *_: (r, c, 0, lane))
    edge = lambda at: pl.BlockSpec((1, BLK, wide), lambda *_: (at, 0, lane))
    return call(
        queries_kernel,
        "finish_queries",
        2,
        [block, rows_spec((2, BLK, wide)), edge(c), edge(0)] + [ANY] * len(done),
        block,
        sds((4, 2, BLK, FULL)),
        alias={5 + i: i for i in range(len(done))},
    )(pos, dqp, back, back_out, corner, *done)


def finish_edges(pos, tail, part, sib, dk, dv):
    row = pl.BlockSpec((1, 2, BLK, FULL), lambda i, p: (3 * i, 0, 0, 0))
    edge = (2, 2, BLK, FULL)
    return call(
        edges_kernel,
        "finish_edges",
        2,
        [rows_spec((1,) + edge)] + [fixed(edge)] * 2 + [ANY] * 2,
        [row] * 2,
        [sds((4, 2, BLK, FULL))] * 2,
        alias={4: 0, 5: 1},
    )(pos, tail, part, sib, dk, dv)


def pairs_of(rows, cols):
    at = lambda s, p: (s % rows) * cols + p
    outer = lambda s: s + 1 if s % 2 else s - 1
    inner = lambda s: s - 1 if s % 2 else s + 1
    cells = [(s, p) for s in range(rows) for p in range(cols)]
    return {
        "right": [(at(s, p), at(s, p + 1)) for s, p in cells if p + 1 < cols],
        "left": [(at(s, p), at(s, p - 1)) for s, p in cells if p > 0],
        "outer": [(at(s, p), at(outer(s), p)) for s, p in cells],
        "inner": [(at(s, p), at(inner(s), p)) for s, p in cells],
        "outer_right": [(at(s, p), at(outer(s), p + 1)) for s, p in cells if p + 1 < cols],
        "outer_left": [(at(s, p), at(outer(s), p - 1)) for s, p in cells if p > 0],
    }


def after(pos, *others):
    return lax.optimization_barrier((pos,) + others)[0]


def on_device(rows, cols, q, k, v, o, do, lse, neighbours, flags):
    pairs = pairs_of(rows, cols)
    send = lambda x, way: lax.ppermute(x, AXES, pairs[way])
    row = lax.axis_index("slit")
    pos = jnp.stack([row % 2, row * 4, lax.axis_index("span") * 2]).astype(jnp.int32)
    lists = (neighbours, flags)

    out, dg0, dg1 = prepare_row(pos, lists, q, do, o, lse)
    halo_out = send(out, "outer")
    pos = after(pos, out)
    inner = 3 - 3 * (row % 2)
    kv = jnp.concatenate([lax.dynamic_slice_in_dim(x, inner, 1, 0) for x in (k, v)], axis=0)
    ks = send(kv, "inner")
    delta1, used1, col1 = prepare_column(pos, lists, q, do, o, lse, 1, [PAIRS])
    pos = after(pos, delta1)
    delta0, used0, *col0 = prepare_column(pos, lists, q, do, o, lse, 0, [FIRST, PAIRS - FIRST])
    from_left = send(after(col1, halo_out, ks, delta0), "right")
    from_right = [send(after(x, halo_out, ks), "left") for x in col0]
    halo_g0 = send(dg1, "outer_right")
    halo_g1 = send(dg0, "outer_left")
    pos = after(pos, delta0)

    *parts, dqp = local(pos, q, do, k, v, ks, lse, (delta0, delta1), (used0, used1))
    pos = after(pos, dqp)
    part_out, ro, rg0, rg1 = outers(pos, k, v, halo_out, halo_g0, halo_g1)
    back_out = send(ro, "outer")
    back_g1 = send(rg0, "outer_left")
    back_g0 = send(rg1, "outer_right")
    pos = after(pos, ro)
    *done, res0 = column(pos, k, v, ks, from_left, parts, (), 0, PAIRS, 0)
    back1 = send(res0, "left")
    pos = after(pos, res0)
    *done, res1 = column(pos, k, v, ks, from_right[0], parts, done, 0, FIRST, 1)
    back0 = send(res1, "right")
    pos = after(pos, res1, back_out, back_g0, back_g1)
    dk, dv, sib, tail, res2 = column(pos, k, v, ks, from_right[1], parts, done, FIRST, PAIRS - FIRST, 1)
    back0_last = send(after(res2, back1), "right")

    dq = finish_queries(pos, dqp, back1, back_out, back_g1, (), 1, 0, PAIRS)
    back_sib = send(sib, "inner")
    pos = after(pos, dq)
    dk, dv = finish_edges(pos, tail, part_out, back_sib, dk, dv)
    pos = after(pos, dk)
    dq = finish_queries(pos, dqp, back0, back_out, back_g0, (dq,), 0, 0, FIRST)
    dq = finish_queries(pos, dqp, back0_last, back_out, back_g0, (dq,), 0, FIRST, PAIRS - FIRST)
    return dq, dk, dv


def solution(mesh):
    tile = P("slit", "span", None, None)
    row = P("slit", "span", None)
    body = functools.partial(on_device, mesh.shape["slit"], mesh.shape["span"])
    return jax.shard_map(
        body,
        mesh=mesh,
        in_specs=(tile,) * 6 + (row,) * 2,
        out_specs=(tile,) * 3,
        check_vma=False,
    )
```

profile of v0, /device:TPU:96, one launch (start us, length us, event | category | flops | bytes accessed | tf_op | source)
XLA Modules:
  0.0 156.2 jit_solution(12868312681974522599)
XLA Ops:
  0.6 1.4 copy.23.lse_ref
  2.1 0.7 pad_add_fusion.pos_ref
  2.7 3.4 %prepare_row.1 = (bf16[2,272,768]{2,1,0:T(8,128)(2,1)}, bf16[1,272,768]{2,1,0:T(8,128)(2,1)}, bf16[1,272,768]{2,1,0:T(8,128)(2,1)}) custom-call(s32[3]{0:T(128)} %pad_add_fusion.pos_ref, s32[4,2,8]{2,1,0:T(2,128)} %near_ref.5, s32[4,2,8]{2,1,0:T(2,128)} %flag_ref.5, bf16[4,2,128,768]{3,2,1,0:T(8,128)(2,1)} %q_ref.7, bf16[4,2,128,768]{3,2,1,0:T(8,128)(2,1)} %do_ref.7, ...), custom_call_target="tpu_custom_call" | custom-call | flops 1 | bytes 1 | tf_op jit(solution)/shard_map/prepare_row/pallas_call | solution.py:373
  6.2 4.8 %collective-permute-start.1 = (bf16[2,272,768]{2,1,0:T(8,128)(2,1)}, bf16[2,272,768]{2,1,0:T(8,128)(2,1)}, u32[]{:S(2)}, u32[]{:S(2)}) collective-permute-start(bf16[2,272,768]{2,1,0:T(8,128)(2,1)} %get-tuple-element.52), channel_id=1, source_target_pairs={{0,120},{1,121},{2,122},{3,123},{4,124},{5,125},{6,126},{7,127},{8... | collective-permute-start | bytes 2506760 | tf_op jit(solution)/shard_map/ppermute | solution.py:495
  11.0 1.2 constant_dynamic-slice_fusion
  12.1 0.9 pad_maximum_fusion
  13.1 0.0 collective-permute-start
  13.1 4.9 %prepare_column.2 = (f32[4,12,128]{2,1,0:T(8,128)}, f32[4,16,128]{2,1,0:T(8,128)}, bf16[4,272,768]{2,1,0:T(8,128)(2,1)}) custom-call(s32[3]{0:T(128)} %pad_add_fusion.pos_ref, s32[4,2,8]{2,1,0:T(2,128)} %near_ref.5, s32[4,2,8]{2,1,0:T(2,128)} %flag_ref.5, bf16[4,2,128,768]{3,2,1,0:T(8,128)(2,1)} %q_ref.7, bf16[4,2,128,768]{3,2,1,0:T(8,128)(2,1)} %do_ref.7, ...), custom_call_target="tpu_custom_call" | custom-call | flops 1 | bytes 1 | tf_op jit(solution)/shard_map/prepare_column/pallas_call | solution.py:359
  18.0 4.9 %prepare_column.3 = (f32[4,12,128]{2,1,0:T(8,128)}, f32[4,16,128]{2,1,0:T(8,128)}, bf16[4,272,512]{2,1,0:T(8,128)(2,1)}, bf16[4,272,256]{2,1,0:T(8,128)(2,1)}) custom-call(s32[3]{0:T(128)} %pad_add_fusion.pos_ref, s32[4,2,8]{2,1,0:T(2,128)} %near_ref.5, s32[4,2,8]{2,1,0:T(2,128)} %flag_ref.5, bf16[4,2,128,768]{3,2,1,0:T(8,128)(2,1)} %q_ref.7, ...), custom_call_target="tpu_custom_call" | custom-call | flops 1 | bytes 1 | tf_op jit(solution)/shard_map/prepare_column/pallas_call | solution.py:359
  22.9 0.0 collective-permute-done.ks_ref
  23.0 0.0 collective-permute-done.1.out_ref
  23.0 2.6 %collective-permute-start.4 = (bf16[4,272,768]{2,1,0:T(8,128)(2,1)}, bf16[4,272,768]{2,1,0:T(8,128)(2,1)}, u32[]{:S(2)}, u32[]{:S(2)}) collective-permute-start(bf16[4,272,768]{2,1,0:T(8,128)(2,1)} %get-tuple-element.67), channel_id=1, source_target_pairs={{0,1},{1,2},{2,3},{3,4},{4,5},{5,6},{6,7},{8,9},{9,10},{10,11},{11... | collective-permute-start | bytes 5013512 | tf_op jit(solution)/shard_map/ppermute | solution.py:495
  25.6 4.1 %collective-permute-start.5 = (bf16[4,272,512]{2,1,0:T(8,128)(2,1)}, bf16[4,272,512]{2,1,0:T(8,128)(2,1)}, u32[]{:S(2)}, u32[]{:S(2)}) collective-permute-start(bf16[4,272,512]{2,1,0:T(8,128)(2,1)} %get-tuple-element.75), channel_id=1, source_target_pairs={{1,0},{2,1},{3,2},{4,3},{5,4},{6,5},{7,6},{9,8},{10,9},{11,10},{12... | collective-permute-start | bytes 3342344 | tf_op jit(solution)/shard_map/ppermute | solution.py:495
  29.7 5.2 %collective-permute-start.2 = (bf16[1,272,768]{2,1,0:T(8,128)(2,1)}, bf16[1,272,768]{2,1,0:T(8,128)(2,1)}, u32[]{:S(2)}, u32[]{:S(2)}) collective-permute-start(bf16[1,272,768]{2,1,0:T(8,128)(2,1)} %get-tuple-element.62), channel_id=1, source_target_pairs={{0,121},{1,122},{2,123},{3,124},{4,125},{5,126},{6,127},{8,17},{9,... | collective-permute-start | bytes 1253384 | tf_op jit(solution)/shard_map/ppermute | solution.py:495
  35.0 4.6 %collective-permute-start.3 = (bf16[1,272,768]{2,1,0:T(8,128)(2,1)}, bf16[1,272,768]{2,1,0:T(8,128)(2,1)}, u32[]{:S(2)}, u32[]{:S(2)}) collective-permute-start(bf16[1,272,768]{2,1,0:T(8,128)(2,1)} %get-tuple-element.63), channel_id=1, source_target_pairs={{1,120},{2,121},{3,122},{4,123},{5,124},{6,125},{7,126},{9,16},{10... | collective-permute-start | bytes 1253384 | tf_op jit(solution)/shard_map/ppermute | solution.py:495
  39.5 1.9 %collective-permute-start.10 = (bf16[4,272,256]{2,1,0:T(8,128)(2,1)}, bf16[4,272,256]{2,1,0:T(8,128)(2,1)}, u32[]{:S(2)}, u32[]{:S(2)}) collective-permute-start(bf16[4,272,256]{2,1,0:T(8,128)(2,1)} %get-tuple-element.86), channel_id=1, source_target_pairs={{1,0},{2,1},{3,2},{4,3},{5,4},{6,5},{7,6},{9,8},{10,9},{11,10},{12... | collective-permute-start | bytes 1671176 | tf_op jit(solution)/shard_map/ppermute | solution.py:495
  41.5 28.4 %local.1 = (f32[4,2,128,768]{3,2,1,0:T(8,128)}, f32[4,2,128,768]{3,2,1,0:T(8,128)}, f32[2,128,768]{2,1,0:T(8,128)}, f32[2,128,768]{2,1,0:T(8,128)}, f32[4,2,128,768]{3,2,1,0:T(8,128)}) custom-call(s32[3]{0:T(128)} %pad_add_fusion.pos_ref, bf16[4,2,128,768]{3,2,1,0:T(8,128)(2,1)} %q_ref.7, bf16[4,2,128,768]{3,2,1,0:T(8,128)(2,1)} %do_ref.7, ...), custom_call_target="tpu_custom_call" | custom-call | flops 1 | bytes 1 | tf_op jit(solution)/shard_map/local/pallas_call | solution.py:387
  69.8 0.0 collective-permute-done.2.dg0_ref
  69.8 0.0 collective-permute-done.3.dg1_ref
  69.8 6.7 %outer_rows.1 = (f32[2,2,128,768]{3,2,1,0:T(8,128)}, bf16[2,128,768]{2,1,0:T(8,128)(2,1)}, bf16[1,128,768]{2,1,0:T(8,128)(2,1)}, bf16[1,128,768]{2,1,0:T(8,128)(2,1)}) custom-call(s32[3]{0:T(128)} %pad_add_fusion.pos_ref, bf16[4,2,128,768]{3,2,1,0:T(8,128)(2,1)} %k_ref.9, bf16[4,2,128,768]{3,2,1,0:T(8,128)(2,1)} %v_ref.9, ...), custom_call_target="tpu_custom_call" | custom-call | flops 1 | bytes 1 | tf_op jit(solution)/shard_map/outer_rows/pallas_call | solution.py:434
  76.5 2.7 %collective-permute-start.6 = (bf16[2,128,768]{2,1,0:T(8,128)(2,1)}, bf16[2,128,768]{2,1,0:T(8,128)(2,1)}, u32[]{:S(2)}, u32[]{:S(2)}) collective-permute-start(bf16[2,128,768]{2,1,0:T(8,128)(2,1)} %get-tuple-element.64), channel_id=1, source_target_pairs={{0,120},{1,121},{2,122},{3,123},{4,124},{5,125},{6,126},{7,127},{8... | collective-permute-start | bytes 1179656 | tf_op jit(solution)/shard_map/ppermute | solution.py:495
  79.2 0.0 collective-permute-done.4.col_ref
  79.2 11.1 %column.3 = (bf16[4,2,128,768]{3,2,1,0:T(8,128)(2,1)}, bf16[4,2,128,768]{3,2,1,0:T(8,128)(2,1)}, bf16[2,2,128,768]{3,2,1,0:T(8,128)(2,1)}, f32[2,2,2,128,768]{4,3,2,1,0:T(8,128)}, bf16[4,128,768]{2,1,0:T(8,128)(2,1)}) custom-call(s32[3]{0:T(128)} %pad_add_fusion.pos_ref, bf16[4,2,128,768]{3,2,1,0:T(8,128)(2,1)} %k_ref.9, bf16[4,2,128,768]{3,2,1,0:T(8,128)(2,1)} %v_ref.9, ...), custom_call_target="tpu_custom_call" | custom-call | flops 1 | bytes 1 | tf_op jit(solution)/shard_map/column/pallas_call | solution.py:406
  90.3 2.6 %collective-permute-start.9 = (bf16[4,128,768]{2,1,0:T(8,128)(2,1)}, bf16[4,128,768]{2,1,0:T(8,128)(2,1)}, u32[]{:S(2)}, u32[]{:S(2)}) collective-permute-start(bf16[4,128,768]{2,1,0:T(8,128)(2,1)} %get-tuple-element.72), channel_id=1, source_target_pairs={{1,0},{2,1},{3,2},{4,3},{5,4},{6,5},{7,6},{9,8},{10,9},{11,10},{12... | collective-permute-start | bytes 2359304 | tf_op jit(solution)/shard_map/ppermute | solution.py:495
  92.9 6.4 %collective-permute-start.7 = (bf16[1,128,768]{2,1,0:T(8,128)(2,1)}, bf16[1,128,768]{2,1,0:T(8,128)(2,1)}, u32[]{:S(2)}, u32[]{:S(2)}) collective-permute-start(bf16[1,128,768]{2,1,0:T(8,128)(2,1)} %get-tuple-element.81), channel_id=1, source_target_pairs={{0,121},{1,122},{2,123},{3,124},{4,125},{5,126},{6,127},{8,17},{9,... | collective-permute-start | bytes 589832 | tf_op jit(solution)/shard_map/ppermute | solution.py:495
  99.3 0.0 collective-permute-done.5.col_ref
  99.3 3.3 %collective-permute-start.8 = (bf16[1,128,768]{2,1,0:T(8,128)(2,1)}, bf16[1,128,768]{2,1,0:T(8,128)(2,1)}, u32[]{:S(2)}, u32[]{:S(2)}) collective-permute-start(bf16[1,128,768]{2,1,0:T(8,128)(2,1)} %get-tuple-element.82), channel_id=1, source_target_pairs={{1,120},{2,121},{3,122},{4,123},{5,124},{6,125},{7,126},{9,16},{10... | collective-permute-start | bytes 589832 | tf_op jit(solution)/shard_map/ppermute | solution.py:495
  102.7 8.5 %column.4 = (bf16[4,2,128,768]{3,2,1,0:T(8,128)(2,1)}, bf16[4,2,128,768]{3,2,1,0:T(8,128)(2,1)}, bf16[2,2,128,768]{3,2,1,0:T(8,128)(2,1)}, f32[2,2,2,128,768]{4,3,2,1,0:T(8,128)}, bf16[4,128,512]{2,1,0:T(8,128)(2,1)}) custom-call(s32[3]{0:T(128)} %pad_add_fusion.pos_ref, ...), custom_call_target="tpu_custom_call", output_to_operand_aliasing={{0}: (9, {}), {1}: (10, {}), {2}: (11, {}), {3}: (12, {})} | custom-call | flops 1 | bytes 1 | tf_op jit(solution)/shard_map/column/pallas_call | solution.py:406
  111.2 0.0 collective-permute-done.7.corner_ref
  111.2 0.0 collective-permute-done.8.corner_ref
  111.2 0.0 collective-permute-done.6.row_ref
  111.2 0.0 collective-permute-done.10.col_ref
  111.3 6.1 %column.5 = (bf16[4,2,128,768]{3,2,1,0:T(8,128)(2,1)}, bf16[4,2,128,768]{3,2,1,0:T(8,128)(2,1)}, bf16[2,2,128,768]{3,2,1,0:T(8,128)(2,1)}, f32[2,2,2,128,768]{4,3,2,1,0:T(8,128)}, bf16[4,128,256]{2,1,0:T(8,128)(2,1)}) custom-call(s32[3]{0:T(128)} %pad_add_fusion.pos_ref, ...), custom_call_target="tpu_custom_call", output_to_operand_aliasing={{0}: (9, {}), {1}: (10, {}), {2}: (11, {}), {3}: (12, {})} | custom-call | flops 1 | bytes 1 | tf_op jit(solution)/shard_map/column/pallas_call | solution.py:406
  117.4 9.4 %collective-permute-start.11 = (bf16[2,2,128,768]{3,2,1,0:T(8,128)(2,1)}, bf16[2,2,128,768]{3,2,1,0:T(8,128)(2,1)}, u32[]{:S(2)}, u32[]{:S(2)}) collective-permute-start(bf16[2,2,128,768]{3,2,1,0:T(8,128)(2,1)} %get-tuple-element.93), channel_id=1, source_target_pairs={{0,8},{1,9},{2,10},{3,11},{4,12},{5,13},{6,14},{7,15},{8,0},{9,1},... | collective-permute-start | bytes 2359304 | tf_op jit(solution)/shard_map/ppermute | solution.py:495
  126.8 1.9 %collective-permute-start.13 = (bf16[4,128,512]{2,1,0:T(8,128)(2,1)}, bf16[4,128,512]{2,1,0:T(8,128)(2,1)}, u32[]{:S(2)}, u32[]{:S(2)}) collective-permute-start(bf16[4,128,512]{2,1,0:T(8,128)(2,1)} %get-tuple-element.80), channel_id=1, source_target_pairs={{0,1},{1,2},{2,3},{3,4},{4,5},{5,6},{6,7},{8,9},{9,10},{10,11},{11... | collective-permute-start | bytes 1572872 | tf_op jit(solution)/shard_map/ppermute | solution.py:495
  128.7 0.0 collective-permute-done.9.back_ref
  128.7 1.9 %collective-permute-start.12 = (bf16[4,128,256]{2,1,0:T(8,128)(2,1)}, bf16[4,128,256]{2,1,0:T(8,128)(2,1)}, u32[]{:S(2)}, u32[]{:S(2)}) collective-permute-start(bf16[4,128,256]{2,1,0:T(8,128)(2,1)} %get-tuple-element.99), channel_id=1, source_target_pairs={{0,1},{1,2},{2,3},{3,4},{4,5},{5,6},{6,7},{8,9},{9,10},{10,11},{11... | collective-permute-start | bytes 786440 | tf_op jit(solution)/shard_map/ppermute | solution.py:495
  130.7 3.3 %finish_queries.3.rest_0_ = bf16[4,2,128,768]{3,2,1,0:T(8,128)(2,1)} custom-call(s32[3]{0:T(128)} %pad_add_fusion.pos_ref, f32[4,2,128,768]{3,2,1,0:T(8,128)} %get-tuple-element.60.dq_ref, bf16[4,128,768]{2,1,0:T(8,128)(2,1)} %collective-permute-done.9.back_ref, bf16[2,128,768]{2,1,0:T(8,128)(2,1)} %collective-permute-done.6.row_ref, ...), custom_call_target="tpu_custom_call" | custom-call | flops 1 | bytes 1 | tf_op jit(solution)/shard_map/finish_queries/pallas_call | solution.py:449
  134.0 0.0 collective-permute-done.11.sib_ref
  134.0 4.3 %finish_edges.1 = (bf16[4,2,128,768]{3,2,1,0:T(8,128)(2,1)}, bf16[4,2,128,768]{3,2,1,0:T(8,128)(2,1)}) custom-call(s32[3]{0:T(128)} %pad_add_fusion.pos_ref, f32[2,2,2,128,768]{4,3,2,1,0:T(8,128)} %get-tuple-element.91.tail_ref, f32[2,2,128,768]{3,2,1,0:T(8,128)} %get-tuple-element.92.part_ref, ...), custom_call_target="tpu_custom_call", output_to_operand_aliasing={{0}: (4, {}), {1}: (5, {})} | custom-call | flops 1 | bytes 1 | tf_op jit(solution)/shard_map/finish_edges/pallas_call | solution.py:463
  138.3 10.3 %collective-permute-done.13.back_ref = bf16[4,128,512]{2,1,0:T(8,128)(2,1)} collective-permute-done((bf16[4,128,512]{2,1,0:T(8,128)(2,1)}, bf16[4,128,512]{2,1,0:T(8,128)(2,1)}, u32[]{:S(2)}, u32[]{:S(2)}) %collective-permute-start.13) | collective-permute-done | bytes 524320 | tf_op jit(solution)/shard_map/ppermute | solution.py:495
  148.6 2.9 %finish_queries.4.rest_0_ = bf16[4,2,128,768]{3,2,1,0:T(8,128)(2,1)} custom-call(s32[3]{0:T(128)} %pad_add_fusion.pos_ref, f32[4,2,128,768]{3,2,1,0:T(8,128)} %get-tuple-element.60.dq_ref, bf16[4,128,512]{2,1,0:T(8,128)(2,1)} %collective-permute-done.13.back_ref, ...), custom_call_target="tpu_custom_call", output_to_operand_aliasing={{}: (5, {})} | custom-call | flops 1 | bytes 1 | tf_op jit(solution)/shard_map/finish_queries/pallas_call | solution.py:449
  151.5 2.0 %collective-permute-done.12.back_ref = bf16[4,128,256]{2,1,0:T(8,128)(2,1)} collective-permute-done((bf16[4,128,256]{2,1,0:T(8,128)(2,1)}, bf16[4,128,256]{2,1,0:T(8,128)(2,1)}, u32[]{:S(2)}, u32[]{:S(2)}) %collective-permute-start.12) | collective-permute-done | bytes 262176 | tf_op jit(solution)/shard_map/ppermute | solution.py:495
  153.6 2.6 %finish_queries.5 = bf16[4,2,128,768]{3,2,1,0:T(8,128)(2,1)} custom-call(s32[3]{0:T(128)} %pad_add_fusion.pos_ref, f32[4,2,128,768]{3,2,1,0:T(8,128)} %get-tuple-element.60.dq_ref, bf16[4,128,256]{2,1,0:T(8,128)(2,1)} %collective-permute-done.12.back_ref, bf16[2,128,768]{2,1,0:T(8,128)(2,1)} %collective-permute-done.6.row_ref, ...), custom_call_target="tpu_custom_call", output_to_operand_aliasing={{}: (5, {})} | custom-call | flops 1 | bytes 1 | tf_op jit(solution)/shard_map/finish_queries/pallas_call | solution.py:449
Async XLA Ops:
  6.2 16.8 %collective-permute-start.1 = (bf16[2,272,768]{2,1,0:T(8,128)(2,1)}, bf16[2,272,768]{2,1,0:T(8,128)(2,1)}, u32[]{:S(2)}, u32[]{:S(2)}) collective-permute-start(bf16[2,272,768]{2,1,0:T(8,128)(2,1)} %get-tuple-element.52), channel_id=1, source_target_pairs={{0,120},{1,121},{2,122},{3,123},{4,124},{5,125},{6,126},{7,127},{8... | collective-permute-start | bytes 2506760 | tf_op jit(solution)/shard_map/ppermute | solution.py:495
  13.1 9.9 %collective-permute-start = (bf16[2,2,128,768]{3,2,1,0:T(8,128)(2,1)}, bf16[2,2,128,768]{3,2,1,0:T(8,128)(2,1)}, u32[]{:S(2)}, u32[]{:S(2)}) collective-permute-start(bf16[2,2,128,768]{3,2,1,0:T(8,128)(2,1)} %pad_maximum_fusion), channel_id=1, source_target_pairs={{0,8},{1,9},{2,10},{3,11},{4,12},{5,13},{6,14},{7,15},{8,0},{9,1},... | collective-permute-start | bytes 2359304 | tf_op jit(solution)/shard_map/ppermute | solution.py:495
  23.0 56.3 %collective-permute-start.4 = (bf16[4,272,768]{2,1,0:T(8,128)(2,1)}, bf16[4,272,768]{2,1,0:T(8,128)(2,1)}, u32[]{:S(2)}, u32[]{:S(2)}) collective-permute-start(bf16[4,272,768]{2,1,0:T(8,128)(2,1)} %get-tuple-element.67), channel_id=1, source_target_pairs={{0,1},{1,2},{2,3},{3,4},{4,5},{5,6},{6,7},{8,9},{9,10},{10,11},{11... | collective-permute-start | bytes 5013512 | tf_op jit(solution)/shard_map/ppermute | solution.py:495
  25.6 73.7 %collective-permute-start.5 = (bf16[4,272,512]{2,1,0:T(8,128)(2,1)}, bf16[4,272,512]{2,1,0:T(8,128)(2,1)}, u32[]{:S(2)}, u32[]{:S(2)}) collective-permute-start(bf16[4,272,512]{2,1,0:T(8,128)(2,1)} %get-tuple-element.75), channel_id=1, source_target_pairs={{1,0},{2,1},{3,2},{4,3},{5,4},{6,5},{7,6},{9,8},{10,9},{11,10},{12... | collective-permute-start | bytes 3342344 | tf_op jit(solution)/shard_map/ppermute | solution.py:495
  29.7 40.1 %collective-permute-start.2 = (bf16[1,272,768]{2,1,0:T(8,128)(2,1)}, bf16[1,272,768]{2,1,0:T(8,128)(2,1)}, u32[]{:S(2)}, u32[]{:S(2)}) collective-permute-start(bf16[1,272,768]{2,1,0:T(8,128)(2,1)} %get-tuple-element.62), channel_id=1, source_target_pairs={{0,121},{1,122},{2,123},{3,124},{4,125},{5,126},{6,127},{8,17},{9,... | collective-permute-start | bytes 1253384 | tf_op jit(solution)/shard_map/ppermute | solution.py:495
  35.0 34.9 %collective-permute-start.3 = (bf16[1,272,768]{2,1,0:T(8,128)(2,1)}, bf16[1,272,768]{2,1,0:T(8,128)(2,1)}, u32[]{:S(2)}, u32[]{:S(2)}) collective-permute-start(bf16[1,272,768]{2,1,0:T(8,128)(2,1)} %get-tuple-element.63), channel_id=1, source_target_pairs={{1,120},{2,121},{3,122},{4,123},{5,124},{6,125},{7,126},{9,16},{10... | collective-permute-start | bytes 1253384 | tf_op jit(solution)/shard_map/ppermute | solution.py:495
  39.5 71.7 %collective-permute-start.10 = (bf16[4,272,256]{2,1,0:T(8,128)(2,1)}, bf16[4,272,256]{2,1,0:T(8,128)(2,1)}, u32[]{:S(2)}, u32[]{:S(2)}) collective-permute-start(bf16[4,272,256]{2,1,0:T(8,128)(2,1)} %get-tuple-element.86), channel_id=1, source_target_pairs={{1,0},{2,1},{3,2},{4,3},{5,4},{6,5},{7,6},{9,8},{10,9},{11,10},{12... | collective-permute-start | bytes 1671176 | tf_op jit(solution)/shard_map/ppermute | solution.py:495
  76.5 34.7 %collective-permute-start.6 = (bf16[2,128,768]{2,1,0:T(8,128)(2,1)}, bf16[2,128,768]{2,1,0:T(8,128)(2,1)}, u32[]{:S(2)}, u32[]{:S(2)}) collective-permute-start(bf16[2,128,768]{2,1,0:T(8,128)(2,1)} %get-tuple-element.64), channel_id=1, source_target_pairs={{0,120},{1,121},{2,122},{3,123},{4,124},{5,125},{6,126},{7,127},{8... | collective-permute-start | bytes 1179656 | tf_op jit(solution)/shard_map/ppermute | solution.py:495
  90.3 38.4 %collective-permute-start.9 = (bf16[4,128,768]{2,1,0:T(8,128)(2,1)}, bf16[4,128,768]{2,1,0:T(8,128)(2,1)}, u32[]{:S(2)}, u32[]{:S(2)}) collective-permute-start(bf16[4,128,768]{2,1,0:T(8,128)(2,1)} %get-tuple-element.72), channel_id=1, source_target_pairs={{1,0},{2,1},{3,2},{4,3},{5,4},{6,5},{7,6},{9,8},{10,9},{11,10},{12... | collective-permute-start | bytes 2359304 | tf_op jit(solution)/shard_map/ppermute | solution.py:495
  92.9 18.3 %collective-permute-start.7 = (bf16[1,128,768]{2,1,0:T(8,128)(2,1)}, bf16[1,128,768]{2,1,0:T(8,128)(2,1)}, u32[]{:S(2)}, u32[]{:S(2)}) collective-permute-start(bf16[1,128,768]{2,1,0:T(8,128)(2,1)} %get-tuple-element.81), channel_id=1, source_target_pairs={{0,121},{1,122},{2,123},{3,124},{4,125},{5,126},{6,127},{8,17},{9,... | collective-permute-start | bytes 589832 | tf_op jit(solution)/shard_map/ppermute | solution.py:495
  99.3 11.9 %collective-permute-start.8 = (bf16[1,128,768]{2,1,0:T(8,128)(2,1)}, bf16[1,128,768]{2,1,0:T(8,128)(2,1)}, u32[]{:S(2)}, u32[]{:S(2)}) collective-permute-start(bf16[1,128,768]{2,1,0:T(8,128)(2,1)} %get-tuple-element.82), channel_id=1, source_target_pairs={{1,120},{2,121},{3,122},{4,123},{5,124},{6,125},{7,126},{9,16},{10... | collective-permute-start | bytes 589832 | tf_op jit(solution)/shard_map/ppermute | solution.py:495
  117.4 16.6 %collective-permute-start.11 = (bf16[2,2,128,768]{3,2,1,0:T(8,128)(2,1)}, bf16[2,2,128,768]{3,2,1,0:T(8,128)(2,1)}, u32[]{:S(2)}, u32[]{:S(2)}) collective-permute-start(bf16[2,2,128,768]{3,2,1,0:T(8,128)(2,1)} %get-tuple-element.93), channel_id=1, source_target_pairs={{0,8},{1,9},{2,10},{3,11},{4,12},{5,13},{6,14},{7,15},{8,0},{9,1},... | collective-permute-start | bytes 2359304 | tf_op jit(solution)/shard_map/ppermute | solution.py:495
  126.8 21.8 %collective-permute-start.13 = (bf16[4,128,512]{2,1,0:T(8,128)(2,1)}, bf16[4,128,512]{2,1,0:T(8,128)(2,1)}, u32[]{:S(2)}, u32[]{:S(2)}) collective-permute-start(bf16[4,128,512]{2,1,0:T(8,128)(2,1)} %get-tuple-element.80), channel_id=1, source_target_pairs={{0,1},{1,2},{2,3},{3,4},{4,5},{5,6},{6,7},{8,9},{9,10},{10,11},{11... | collective-permute-start | bytes 1572872 | tf_op jit(solution)/shard_map/ppermute | solution.py:495
  128.7 24.8 %collective-permute-start.12 = (bf16[4,128,256]{2,1,0:T(8,128)(2,1)}, bf16[4,128,256]{2,1,0:T(8,128)(2,1)}, u32[]{:S(2)}, u32[]{:S(2)}) collective-permute-start(bf16[4,128,256]{2,1,0:T(8,128)(2,1)} %get-tuple-element.99), channel_id=1, source_target_pairs={{0,1},{1,2},{2,3},{3,4},{4,5},{5,6},{6,7},{8,9},{9,10},{10,11},{11... | collective-permute-start | bytes 786440 | tf_op jit(solution)/shard_map/ppermute | solution.py:495
where the time goes:
time: 159 us; the launch traced here: 156 us
  Pallas kernels  87.2 us (55%)
  starting transfers between devices  51.6 us (32%)
  waiting for transfers between devices  12.3 us (8%)
  local copies, waits for them, and re-layouts  2.6 us (2%)
  other arithmetic  1.6 us (1%)
    ppermute x14, starting transfers between devices, on_device(): send = lambda x, way: lax.ppermute(x, AXES, pairs[way])  51.6 us
    pallas_call x1, Pallas kernels, local(): call(local_kernel, 'local', PAIRS, [lanes_spec(TILES)] * 4 + [lanes_spec(...  28.4 us
    pallas_call x3, Pallas kernels, column(): call(functools.partial(column_kernel, side=side, sub=sub), 'column', coun...  25.8 us
    ppermute x14, waiting for transfers between devices, on_device(): send = lambda x, way: lax.ppermute(x, AXES, pairs[way])  12.3 us
    pallas_call x2, Pallas kernels, prepare_column(): call(functools.partial(prepare_column_kernel, c=c), 'prepare_column', 4,...  9.85 us
    pallas_call x3, Pallas kernels, finish_queries(): call(queries_kernel, 'finish_queries', 2, [block, rows_spec((2, BLK, wide...  8.88 us
    pallas_call x1, Pallas kernels, outers(): call(outer_kernel, 'outer_rows', PAIRS // SUB, [outer] * 2 + [lanes_spec(...  6.69 us
    pallas_call x1, Pallas kernels, finish_edges(): call(edges_kernel, 'finish_edges', 2, [rows_spec((1,) + edge)] + [fixed(e...  4.3 us
  transfers between devices with their start and end apart: 14, of which 2 were waited for; matrix products, arithmetic and copies ran while one was open for 1% of the time, Pallas kernels for 52%

commit v1 on v0

--- a/solution.py
+++ b/solution.py
@@ -506,10 +506,11 @@
     delta1, used1, col1 = prepare_column(pos, lists, q, do, o, lse, 1, [PAIRS])
     pos = after(pos, delta1)
     delta0, used0, *col0 = prepare_column(pos, lists, q, do, o, lse, 0, [FIRST, PAIRS - FIRST])
-    from_left = send(after(col1, halo_out, ks, delta0), "right")
-    from_right = [send(after(x, halo_out, ks), "left") for x in col0]
+    from_left = send(after(col1, ks), "right")
     halo_g0 = send(dg1, "outer_right")
     halo_g1 = send(dg0, "outer_left")
+    ready = (halo_out, ks, halo_g0, halo_g1)
+    from_right = [send(after(x, *ready), "left") for x in col0]
     pos = after(pos, delta0)
 
     *parts, dqp = local(pos, q, do, k, v, ks, lse, (delta0, delta1), (used0, used1))

time: 159 us -> 157 us (0.987)
  starting transfers between devices: 51.6 us -> 54.3 us
  waiting for transfers between devices: 12.3 us -> 9.99 us
    ppermute x14, starting transfers between devices: 51.6 us -> 54.3 us  [on_device(): send = lambda x, way: lax.ppermute(x, AXES, pairs[way])]
    ppermute x14, waiting for transfers between devices: 12.3 us -> 9.99 us  [on_device(): send = lambda x, way: lax.ppermute(x, AXES, pairs[way])]
  transfers between devices with their start and end apart: 14 -> 14, of which waited for: 2 -> 4; matrix products, arithmetic and copies ran while one was open for 1% -> 1% of each run, Pallas kernels for 52% -> 54%
where the time goes in v1:
time: 157 us; the launch traced here: 156 us
  Pallas kernels  87.2 us (56%)
  starting transfers between devices  54.3 us (35%)
  waiting for transfers between devices  9.99 us (6%)
  local copies, waits for them, and re-layouts  1.81 us (1%)
    ppermute x14, starting transfers between devices, on_device(): send = lambda x, way: lax.ppermute(x, AXES, pairs[way])  54.3 us
    pallas_call x1, Pallas kernels, local(): call(local_kernel, 'local', PAIRS, [lanes_spec(TILES)] * 4 + [lanes_spec(...  28.3 us
    pallas_call x3, Pallas kernels, column(): call(functools.partial(column_kernel, side=side, sub=sub), 'column', coun...  25.8 us
    ppermute x14, waiting for transfers between devices, on_device(): send = lambda x, way: lax.ppermute(x, AXES, pairs[way])  9.99 us
    pallas_call x2, Pallas kernels, prepare_column(): call(functools.partial(prepare_column_kernel, c=c), 'prepare_column', 4,...  9.83 us
    pallas_call x3, Pallas kernels, finish_queries(): call(queries_kernel, 'finish_queries', 2, [block, rows_spec((2, BLK, wide...  8.88 us
    pallas_call x1, Pallas kernels, outers(): call(outer_kernel, 'outer_rows', PAIRS // SUB, [outer] * 2 + [lanes_spec(...  6.62 us
    pallas_call x1, Pallas kernels, finish_edges(): call(edges_kernel, 'finish_edges', 2, [rows_spec((1,) + edge)] + [fixed(e...  4.3 us
  transfers between devices with their start and end apart: 14, of which 4 were waited for; matrix products, arithmetic and copies ran while one was open for 1% of the time, Pallas kernels for 54%

profile of v1, /device:TPU:96, one launch (start us, length us, event | category | flops | bytes accessed | tf_op | source)
XLA Modules:
  0.0 155.6 jit_solution(10306687968909497239)
XLA Ops:
  0.6 0.0 copy-start
  0.7 1.2 constant_dynamic-slice_fusion
  1.8 0.9 pad_maximum_fusion
  2.8 0.0 collective-permute-start
  2.8 0.0 copy-done
  2.8 0.6 copy.23.lse_ref
  3.4 0.6 pad_add_fusion.pos_ref
  4.0 3.4 %prepare_row.1 = (bf16[2,272,768]{2,1,0:T(8,128)(2,1)}, bf16[1,272,768]{2,1,0:T(8,128)(2,1)}, bf16[1,272,768]{2,1,0:T(8,128)(2,1)}) custom-call(s32[3]{0:T(128)} %pad_add_fusion.pos_ref, s32[4,2,8]{2,1,0:T(2,128)} %near_ref.5, s32[4,2,8]{2,1,0:T(2,128)} %flag_ref.5, bf16[4,2,128,768]{3,2,1,0:T(8,128)(2,1)} %q_ref.7, bf16[4,2,128,768]{3,2,1,0:T(8,128)(2,1)} %do_ref.7, ...), custom_call_target="tpu_custom_call" | custom-call | flops 1 | bytes 1 | tf_op jit(solution)/shard_map/prepare_row/pallas_call | solution.py:373
  7.4 5.5 %collective-permute-start.1 = (bf16[2,272,768]{2,1,0:T(8,128)(2,1)}, bf16[2,272,768]{2,1,0:T(8,128)(2,1)}, u32[]{:S(2)}, u32[]{:S(2)}) collective-permute-start(bf16[2,272,768]{2,1,0:T(8,128)(2,1)} %get-tuple-element.52), channel_id=1, source_target_pairs={{0,120},{1,121},{2,122},{3,123},{4,124},{5,125},{6,126},{7,127},{8... | collective-permute-start | bytes 2506760 | tf_op jit(solution)/shard_map/ppermute | solution.py:495
  12.9 4.9 %prepare_column.2 = (f32[4,12,128]{2,1,0:T(8,128)}, f32[4,16,128]{2,1,0:T(8,128)}, bf16[4,272,768]{2,1,0:T(8,128)(2,1)}) custom-call(s32[3]{0:T(128)} %pad_add_fusion.pos_ref, s32[4,2,8]{2,1,0:T(2,128)} %near_ref.5, s32[4,2,8]{2,1,0:T(2,128)} %flag_ref.5, bf16[4,2,128,768]{3,2,1,0:T(8,128)(2,1)} %q_ref.7, bf16[4,2,128,768]{3,2,1,0:T(8,128)(2,1)} %do_ref.7, ...), custom_call_target="tpu_custom_call" | custom-call | flops 1 | bytes 1 | tf_op jit(solution)/shard_map/prepare_column/pallas_call | solution.py:359
  17.9 0.0 collective-permute-done.ks_ref
  17.9 2.6 %collective-permute-start.4 = (bf16[4,272,768]{2,1,0:T(8,128)(2,1)}, bf16[4,272,768]{2,1,0:T(8,128)(2,1)}, u32[]{:S(2)}, u32[]{:S(2)}) collective-permute-start(bf16[4,272,768]{2,1,0:T(8,128)(2,1)} %get-tuple-element.67), channel_id=1, source_target_pairs={{0,1},{1,2},{2,3},{3,4},{4,5},{5,6},{6,7},{8,9},{9,10},{10,11},{11... | collective-permute-start | bytes 5013512 | tf_op jit(solution)/shard_map/ppermute | solution.py:495
  20.5 1.9 %collective-permute-start.2 = (bf16[1,272,768]{2,1,0:T(8,128)(2,1)}, bf16[1,272,768]{2,1,0:T(8,128)(2,1)}, u32[]{:S(2)}, u32[]{:S(2)}) collective-permute-start(bf16[1,272,768]{2,1,0:T(8,128)(2,1)} %get-tuple-element.62), channel_id=1, source_target_pairs={{0,121},{1,122},{2,123},{3,124},{4,125},{5,126},{6,127},{8,17},{9,... | collective-permute-start | bytes 1253384 | tf_op jit(solution)/shard_map/ppermute | solution.py:495
  22.4 7.9 %collective-permute-start.3 = (bf16[1,272,768]{2,1,0:T(8,128)(2,1)}, bf16[1,272,768]{2,1,0:T(8,128)(2,1)}, u32[]{:S(2)}, u32[]{:S(2)}) collective-permute-start(bf16[1,272,768]{2,1,0:T(8,128)(2,1)} %get-tuple-element.63), channel_id=1, source_target_pairs={{1,120},{2,121},{3,122},{4,123},{5,124},{6,125},{7,126},{9,16},{10... | collective-permute-start | bytes 1253384 | tf_op jit(solution)/shard_map/ppermute | solution.py:495
  30.3 4.9 %prepare_column.3 = (f32[4,12,128]{2,1,0:T(8,128)}, f32[4,16,128]{2,1,0:T(8,128)}, bf16[4,272,512]{2,1,0:T(8,128)(2,1)}, bf16[4,272,256]{2,1,0:T(8,128)(2,1)}) custom-call(s32[3]{0:T(128)} %pad_add_fusion.pos_ref, s32[4,2,8]{2,1,0:T(2,128)} %near_ref.5, s32[4,2,8]{2,1,0:T(2,128)} %flag_ref.5, bf16[4,2,128,768]{3,2,1,0:T(8,128)(2,1)} %q_ref.7, ...), custom_call_target="tpu_custom_call" | custom-call | flops 1 | bytes 1 | tf_op jit(solution)/shard_map/prepare_column/pallas_call | solution.py:359
  35.2 2.5 %collective-permute-done.2.dg0_ref = bf16[1,272,768]{2,1,0:T(8,128)(2,1)} collective-permute-done((bf16[1,272,768]{2,1,0:T(8,128)(2,1)}, bf16[1,272,768]{2,1,0:T(8,128)(2,1)}, u32[]{:S(2)}, u32[]{:S(2)}) %collective-permute-start.2) | collective-permute-done | bytes 417824 | tf_op jit(solution)/shard_map/ppermute | solution.py:495
  37.7 0.5 collective-permute-done.3.dg1_ref
  38.2 0.0 collective-permute-done.1.out_ref
  38.2 6.1 %collective-permute-start.5 = (bf16[4,272,512]{2,1,0:T(8,128)(2,1)}, bf16[4,272,512]{2,1,0:T(8,128)(2,1)}, u32[]{:S(2)}, u32[]{:S(2)}) collective-permute-start(bf16[4,272,512]{2,1,0:T(8,128)(2,1)} %get-tuple-element.75), channel_id=1, source_target_pairs={{1,0},{2,1},{3,2},{4,3},{5,4},{6,5},{7,6},{9,8},{10,9},{11,10},{12... | collective-permute-start | bytes 3342344 | tf_op jit(solution)/shard_map/ppermute | solution.py:495
  44.3 4.5 %collective-permute-start.10 = (bf16[4,272,256]{2,1,0:T(8,128)(2,1)}, bf16[4,272,256]{2,1,0:T(8,128)(2,1)}, u32[]{:S(2)}, u32[]{:S(2)}) collective-permute-start(bf16[4,272,256]{2,1,0:T(8,128)(2,1)} %get-tuple-element.86), channel_id=1, source_target_pairs={{1,0},{2,1},{3,2},{4,3},{5,4},{6,5},{7,6},{9,8},{10,9},{11,10},{12... | collective-permute-start | bytes 1671176 | tf_op jit(solution)/shard_map/ppermute | solution.py:495
  48.8 28.3 %local.1 = (f32[4,2,128,768]{3,2,1,0:T(8,128)}, f32[4,2,128,768]{3,2,1,0:T(8,128)}, f32[2,128,768]{2,1,0:T(8,128)}, f32[2,128,768]{2,1,0:T(8,128)}, f32[4,2,128,768]{3,2,1,0:T(8,128)}) custom-call(s32[3]{0:T(128)} %pad_add_fusion.pos_ref, bf16[4,2,128,768]{3,2,1,0:T(8,128)(2,1)} %q_ref.7, bf16[4,2,128,768]{3,2,1,0:T(8,128)(2,1)} %do_ref.7, ...), custom_call_target="tpu_custom_call" | custom-call | flops 1 | bytes 1 | tf_op jit(solution)/shard_map/local/pallas_call | solution.py:387
  77.1 6.6 %outer_rows.1 = (f32[2,2,128,768]{3,2,1,0:T(8,128)}, bf16[2,128,768]{2,1,0:T(8,128)(2,1)}, bf16[1,128,768]{2,1,0:T(8,128)(2,1)}, bf16[1,128,768]{2,1,0:T(8,128)(2,1)}) custom-call(s32[3]{0:T(128)} %pad_add_fusion.pos_ref, bf16[4,2,128,768]{3,2,1,0:T(8,128)(2,1)} %k_ref.9, bf16[4,2,128,768]{3,2,1,0:T(8,128)(2,1)} %v_ref.9, ...), custom_call_target="tpu_custom_call" | custom-call | flops 1 | bytes 1 | tf_op jit(solution)/shard_map/outer_rows/pallas_call | solution.py:434
  83.7 1.1 collective-permute-start.6
  84.9 0.0 collective-permute-done.4.col_ref
  84.9 11.2 %column.3 = (bf16[4,2,128,768]{3,2,1,0:T(8,128)(2,1)}, bf16[4,2,128,768]{3,2,1,0:T(8,128)(2,1)}, bf16[2,2,128,768]{3,2,1,0:T(8,128)(2,1)}, f32[2,2,2,128,768]{4,3,2,1,0:T(8,128)}, bf16[4,128,768]{2,1,0:T(8,128)(2,1)}) custom-call(s32[3]{0:T(128)} %pad_add_fusion.pos_ref, bf16[4,2,128,768]{3,2,1,0:T(8,128)(2,1)} %k_ref.9, bf16[4,2,128,768]{3,2,1,0:T(8,128)(2,1)} %v_ref.9, ...), custom_call_target="tpu_custom_call" | custom-call | flops 1 | bytes 1 | tf_op jit(solution)/shard_map/column/pallas_call | solution.py:406
  96.0 3.2 %collective-permute-start.9 = (bf16[4,128,768]{2,1,0:T(8,128)(2,1)}, bf16[4,128,768]{2,1,0:T(8,128)(2,1)}, u32[]{:S(2)}, u32[]{:S(2)}) collective-permute-start(bf16[4,128,768]{2,1,0:T(8,128)(2,1)} %get-tuple-element.72), channel_id=1, source_target_pairs={{1,0},{2,1},{3,2},{4,3},{5,4},{6,5},{7,6},{9,8},{10,9},{11,10},{12... | collective-permute-start | bytes 2359304 | tf_op jit(solution)/shard_map/ppermute | solution.py:495
  99.2 6.3 %collective-permute-start.7 = (bf16[1,128,768]{2,1,0:T(8,128)(2,1)}, bf16[1,128,768]{2,1,0:T(8,128)(2,1)}, u32[]{:S(2)}, u32[]{:S(2)}) collective-permute-start(bf16[1,128,768]{2,1,0:T(8,128)(2,1)} %get-tuple-element.81), channel_id=1, source_target_pairs={{0,121},{1,122},{2,123},{3,124},{4,125},{5,126},{6,127},{8,17},{9,... | collective-permute-start | bytes 589832 | tf_op jit(solution)/shard_map/ppermute | solution.py:495
  105.5 0.0 collective-permute-done.5.col_ref
  105.5 3.5 %collective-permute-start.8 = (bf16[1,128,768]{2,1,0:T(8,128)(2,1)}, bf16[1,128,768]{2,1,0:T(8,128)(2,1)}, u32[]{:S(2)}, u32[]{:S(2)}) collective-permute-start(bf16[1,128,768]{2,1,0:T(8,128)(2,1)} %get-tuple-element.82), channel_id=1, source_target_pairs={{1,120},{2,121},{3,122},{4,123},{5,124},{6,125},{7,126},{9,16},{10... | collective-permute-start | bytes 589832 | tf_op jit(solution)/shard_map/ppermute | solution.py:495
  109.0 8.5 %column.4 = (bf16[4,2,128,768]{3,2,1,0:T(8,128)(2,1)}, bf16[4,2,128,768]{3,2,1,0:T(8,128)(2,1)}, bf16[2,2,128,768]{3,2,1,0:T(8,128)(2,1)}, f32[2,2,2,128,768]{4,3,2,1,0:T(8,128)}, bf16[4,128,512]{2,1,0:T(8,128)(2,1)}) custom-call(s32[3]{0:T(128)} %pad_add_fusion.pos_ref, ...), custom_call_target="tpu_custom_call", output_to_operand_aliasing={{0}: (9, {}), {1}: (10, {}), {2}: (11, {}), {3}: (12, {})} | custom-call | flops 1 | bytes 1 | tf_op jit(solution)/shard_map/column/pallas_call | solution.py:406
  117.6 0.0 collective-permute-done.7.corner_ref
  117.6 0.0 collective-permute-done.8.corner_ref
  117.6 0.0 collective-permute-done.6.row_ref
  117.6 0.0 collective-permute-done.10.col_ref
  117.6 6.1 %column.5 = (bf16[4,2,128,768]{3,2,1,0:T(8,128)(2,1)}, bf16[4,2,128,768]{3,2,1,0:T(8,128)(2,1)}, bf16[2,2,128,768]{3,2,1,0:T(8,128)(2,1)}, f32[2,2,2,128,768]{4,3,2,1,0:T(8,128)}, bf16[4,128,256]{2,1,0:T(8,128)(2,1)}) custom-call(s32[3]{0:T(128)} %pad_add_fusion.pos_ref, ...), custom_call_target="tpu_custom_call", output_to_operand_aliasing={{0}: (9, {}), {1}: (10, {}), {2}: (11, {}), {3}: (12, {})} | custom-call | flops 1 | bytes 1 | tf_op jit(solution)/shard_map/column/pallas_call | solution.py:406
  123.7 6.8 %collective-permute-start.11 = (bf16[2,2,128,768]{3,2,1,0:T(8,128)(2,1)}, bf16[2,2,128,768]{3,2,1,0:T(8,128)(2,1)}, u32[]{:S(2)}, u32[]{:S(2)}) collective-permute-start(bf16[2,2,128,768]{3,2,1,0:T(8,128)(2,1)} %get-tuple-element.93), channel_id=1, source_target_pairs={{0,8},{1,9},{2,10},{3,11},{4,12},{5,13},{6,14},{7,15},{8,0},{9,1},... | collective-permute-start | bytes 2359304 | tf_op jit(solution)/shard_map/ppermute | solution.py:495
  130.5 3.0 %collective-permute-start.13 = (bf16[4,128,512]{2,1,0:T(8,128)(2,1)}, bf16[4,128,512]{2,1,0:T(8,128)(2,1)}, u32[]{:S(2)}, u32[]{:S(2)}) collective-permute-start(bf16[4,128,512]{2,1,0:T(8,128)(2,1)} %get-tuple-element.80), channel_id=1, source_target_pairs={{0,1},{1,2},{2,3},{3,4},{4,5},{5,6},{6,7},{8,9},{9,10},{10,11},{11... | collective-permute-start | bytes 1572872 | tf_op jit(solution)/shard_map/ppermute | solution.py:495
  133.5 0.0 collective-permute-done.9.back_ref
  133.6 1.9 %collective-permute-start.12 = (bf16[4,128,256]{2,1,0:T(8,128)(2,1)}, bf16[4,128,256]{2,1,0:T(8,128)(2,1)}, u32[]{:S(2)}, u32[]{:S(2)}) collective-permute-start(bf16[4,128,256]{2,1,0:T(8,128)(2,1)} %get-tuple-element.99), channel_id=1, source_target_pairs={{0,1},{1,2},{2,3},{3,4},{4,5},{5,6},{6,7},{8,9},{9,10},{10,11},{11... | collective-permute-start | bytes 786440 | tf_op jit(solution)/shard_map/ppermute | solution.py:495
  135.5 3.3 %finish_queries.3.rest_0_ = bf16[4,2,128,768]{3,2,1,0:T(8,128)(2,1)} custom-call(s32[3]{0:T(128)} %pad_add_fusion.pos_ref, f32[4,2,128,768]{3,2,1,0:T(8,128)} %get-tuple-element.60.dq_ref, bf16[4,128,768]{2,1,0:T(8,128)(2,1)} %collective-permute-done.9.back_ref, bf16[2,128,768]{2,1,0:T(8,128)(2,1)} %collective-permute-done.6.row_ref, ...), custom_call_target="tpu_custom_call" | custom-call | flops 1 | bytes 1 | tf_op jit(solution)/shard_map/finish_queries/pallas_call | solution.py:449
  138.8 0.0 collective-permute-done.11.sib_ref
  138.8 4.3 %finish_edges.1 = (bf16[4,2,128,768]{3,2,1,0:T(8,128)(2,1)}, bf16[4,2,128,768]{3,2,1,0:T(8,128)(2,1)}) custom-call(s32[3]{0:T(128)} %pad_add_fusion.pos_ref, f32[2,2,2,128,768]{4,3,2,1,0:T(8,128)} %get-tuple-element.91.tail_ref, f32[2,2,128,768]{3,2,1,0:T(8,128)} %get-tuple-element.92.part_ref, ...), custom_call_target="tpu_custom_call", output_to_operand_aliasing={{0}: (4, {}), {1}: (5, {})} | custom-call | flops 1 | bytes 1 | tf_op jit(solution)/shard_map/finish_edges/pallas_call | solution.py:463
  143.1 5.3 %collective-permute-done.13.back_ref = bf16[4,128,512]{2,1,0:T(8,128)(2,1)} collective-permute-done((bf16[4,128,512]{2,1,0:T(8,128)(2,1)}, bf16[4,128,512]{2,1,0:T(8,128)(2,1)}, u32[]{:S(2)}, u32[]{:S(2)}) %collective-permute-start.13) | collective-permute-done | bytes 524320 | tf_op jit(solution)/shard_map/ppermute | solution.py:495
  148.4 2.9 %finish_queries.4.rest_0_ = bf16[4,2,128,768]{3,2,1,0:T(8,128)(2,1)} custom-call(s32[3]{0:T(128)} %pad_add_fusion.pos_ref, f32[4,2,128,768]{3,2,1,0:T(8,128)} %get-tuple-element.60.dq_ref, bf16[4,128,512]{2,1,0:T(8,128)(2,1)} %collective-permute-done.13.back_ref, ...), custom_call_target="tpu_custom_call", output_to_operand_aliasing={{}: (5, {})} | custom-call | flops 1 | bytes 1 | tf_op jit(solution)/shard_map/finish_queries/pallas_call | solution.py:449
  151.3 1.7 %collective-permute-done.12.back_ref = bf16[4,128,256]{2,1,0:T(8,128)(2,1)} collective-permute-done((bf16[4,128,256]{2,1,0:T(8,128)(2,1)}, bf16[4,128,256]{2,1,0:T(8,128)(2,1)}, u32[]{:S(2)}, u32[]{:S(2)}) %collective-permute-start.12) | collective-permute-done | bytes 262176 | tf_op jit(solution)/shard_map/ppermute | solution.py:495
  153.0 2.6 %finish_queries.5 = bf16[4,2,128,768]{3,2,1,0:T(8,128)(2,1)} custom-call(s32[3]{0:T(128)} %pad_add_fusion.pos_ref, f32[4,2,128,768]{3,2,1,0:T(8,128)} %get-tuple-element.60.dq_ref, bf16[4,128,256]{2,1,0:T(8,128)(2,1)} %collective-permute-done.12.back_ref, bf16[2,128,768]{2,1,0:T(8,128)(2,1)} %collective-permute-done.6.row_ref, ...), custom_call_target="tpu_custom_call", output_to_operand_aliasing={{}: (5, {})} | custom-call | flops 1 | bytes 1 | tf_op jit(solution)/shard_map/finish_queries/pallas_call | solution.py:449
Async XLA Ops:
  0.6 2.1 %copy-start = (f32[4,2,12,128]{3,1,2,0:T(2,128)S(1)}, f32[4,2,12,128]{3,1,2,0:T(2,128)}, u32[]{:S(2)}) copy-start(f32[4,2,12,128]{3,1,2,0:T(2,128)} %param.13) | copy-start | bytes 147460
  2.8 15.1 %collective-permute-start = (bf16[2,2,128,768]{3,2,1,0:T(8,128)(2,1)}, bf16[2,2,128,768]{3,2,1,0:T(8,128)(2,1)}, u32[]{:S(2)}, u32[]{:S(2)}) collective-permute-start(bf16[2,2,128,768]{3,2,1,0:T(8,128)(2,1)} %pad_maximum_fusion), channel_id=1, source_target_pairs={{0,8},{1,9},{2,10},{3,11},{4,12},{5,13},{6,14},{7,15},{8,0},{9,1},... | collective-permute-start | bytes 2359304 | tf_op jit(solution)/shard_map/ppermute | solution.py:495
  7.4 30.7 %collective-permute-start.1 = (bf16[2,272,768]{2,1,0:T(8,128)(2,1)}, bf16[2,272,768]{2,1,0:T(8,128)(2,1)}, u32[]{:S(2)}, u32[]{:S(2)}) collective-permute-start(bf16[2,272,768]{2,1,0:T(8,128)(2,1)} %get-tuple-element.52), channel_id=1, source_target_pairs={{0,120},{1,121},{2,122},{3,123},{4,124},{5,125},{6,126},{7,127},{8... | collective-permute-start | bytes 2506760 | tf_op jit(solution)/shard_map/ppermute | solution.py:495
  17.9 67.0 %collective-permute-start.4 = (bf16[4,272,768]{2,1,0:T(8,128)(2,1)}, bf16[4,272,768]{2,1,0:T(8,128)(2,1)}, u32[]{:S(2)}, u32[]{:S(2)}) collective-permute-start(bf16[4,272,768]{2,1,0:T(8,128)(2,1)} %get-tuple-element.67), channel_id=1, source_target_pairs={{0,1},{1,2},{2,3},{3,4},{4,5},{5,6},{6,7},{8,9},{9,10},{10,11},{11... | collective-permute-start | bytes 5013512 | tf_op jit(solution)/shard_map/ppermute | solution.py:495
  20.5 17.2 %collective-permute-start.2 = (bf16[1,272,768]{2,1,0:T(8,128)(2,1)}, bf16[1,272,768]{2,1,0:T(8,128)(2,1)}, u32[]{:S(2)}, u32[]{:S(2)}) collective-permute-start(bf16[1,272,768]{2,1,0:T(8,128)(2,1)} %get-tuple-element.62), channel_id=1, source_target_pairs={{0,121},{1,122},{2,123},{3,124},{4,125},{5,126},{6,127},{8,17},{9,... | collective-permute-start | bytes 1253384 | tf_op jit(solution)/shard_map/ppermute | solution.py:495
  22.4 15.8 %collective-permute-start.3 = (bf16[1,272,768]{2,1,0:T(8,128)(2,1)}, bf16[1,272,768]{2,1,0:T(8,128)(2,1)}, u32[]{:S(2)}, u32[]{:S(2)}) collective-permute-start(bf16[1,272,768]{2,1,0:T(8,128)(2,1)} %get-tuple-element.63), channel_id=1, source_target_pairs={{1,120},{2,121},{3,122},{4,123},{5,124},{6,125},{7,126},{9,16},{10... | collective-permute-start | bytes 1253384 | tf_op jit(solution)/shard_map/ppermute | solution.py:495
  38.2 67.3 %collective-permute-start.5 = (bf16[4,272,512]{2,1,0:T(8,128)(2,1)}, bf16[4,272,512]{2,1,0:T(8,128)(2,1)}, u32[]{:S(2)}, u32[]{:S(2)}) collective-permute-start(bf16[4,272,512]{2,1,0:T(8,128)(2,1)} %get-tuple-element.75), channel_id=1, source_target_pairs={{1,0},{2,1},{3,2},{4,3},{5,4},{6,5},{7,6},{9,8},{10,9},{11,10},{12... | collective-permute-start | bytes 3342344 | tf_op jit(solution)/shard_map/ppermute | solution.py:495
  44.3 73.3 %collective-permute-start.10 = (bf16[4,272,256]{2,1,0:T(8,128)(2,1)}, bf16[4,272,256]{2,1,0:T(8,128)(2,1)}, u32[]{:S(2)}, u32[]{:S(2)}) collective-permute-start(bf16[4,272,256]{2,1,0:T(8,128)(2,1)} %get-tuple-element.86), channel_id=1, source_target_pairs={{1,0},{2,1},{3,2},{4,3},{5,4},{6,5},{7,6},{9,8},{10,9},{11,10},{12... | collective-permute-start | bytes 1671176 | tf_op jit(solution)/shard_map/ppermute | solution.py:495
  83.7 33.8 %collective-permute-start.6 = (bf16[2,128,768]{2,1,0:T(8,128)(2,1)}, bf16[2,128,768]{2,1,0:T(8,128)(2,1)}, u32[]{:S(2)}, u32[]{:S(2)}) collective-permute-start(bf16[2,128,768]{2,1,0:T(8,128)(2,1)} %get-tuple-element.64), channel_id=1, source_target_pairs={{0,120},{1,121},{2,122},{3,123},{4,124},{5,125},{6,126},{7,127},{8... | collective-permute-start | bytes 1179656 | tf_op jit(solution)/shard_map/ppermute | solution.py:495
  96.0 37.5 %collective-permute-start.9 = (bf16[4,128,768]{2,1,0:T(8,128)(2,1)}, bf16[4,128,768]{2,1,0:T(8,128)(2,1)}, u32[]{:S(2)}, u32[]{:S(2)}) collective-permute-start(bf16[4,128,768]{2,1,0:T(8,128)(2,1)} %get-tuple-element.72), channel_id=1, source_target_pairs={{1,0},{2,1},{3,2},{4,3},{5,4},{6,5},{7,6},{9,8},{10,9},{11,10},{12... | collective-permute-start | bytes 2359304 | tf_op jit(solution)/shard_map/ppermute | solution.py:495
  99.2 18.3 %collective-permute-start.7 = (bf16[1,128,768]{2,1,0:T(8,128)(2,1)}, bf16[1,128,768]{2,1,0:T(8,128)(2,1)}, u32[]{:S(2)}, u32[]{:S(2)}) collective-permute-start(bf16[1,128,768]{2,1,0:T(8,128)(2,1)} %get-tuple-element.81), channel_id=1, source_target_pairs={{0,121},{1,122},{2,123},{3,124},{4,125},{5,126},{6,127},{8,17},{9,... | collective-permute-start | bytes 589832 | tf_op jit(solution)/shard_map/ppermute | solution.py:495
  105.5 12.0 %collective-permute-start.8 = (bf16[1,128,768]{2,1,0:T(8,128)(2,1)}, bf16[1,128,768]{2,1,0:T(8,128)(2,1)}, u32[]{:S(2)}, u32[]{:S(2)}) collective-permute-start(bf16[1,128,768]{2,1,0:T(8,128)(2,1)} %get-tuple-element.82), channel_id=1, source_target_pairs={{1,120},{2,121},{3,122},{4,123},{5,124},{6,125},{7,126},{9,16},{10... | collective-permute-start | bytes 589832 | tf_op jit(solution)/shard_map/ppermute | solution.py:495
  123.7 15.1 %collective-permute-start.11 = (bf16[2,2,128,768]{3,2,1,0:T(8,128)(2,1)}, bf16[2,2,128,768]{3,2,1,0:T(8,128)(2,1)}, u32[]{:S(2)}, u32[]{:S(2)}) collective-permute-start(bf16[2,2,128,768]{3,2,1,0:T(8,128)(2,1)} %get-tuple-element.93), channel_id=1, source_target_pairs={{0,8},{1,9},{2,10},{3,11},{4,12},{5,13},{6,14},{7,15},{8,0},{9,1},... | collective-permute-start | bytes 2359304 | tf_op jit(solution)/shard_map/ppermute | solution.py:495
  130.5 17.9 %collective-permute-start.13 = (bf16[4,128,512]{2,1,0:T(8,128)(2,1)}, bf16[4,128,512]{2,1,0:T(8,128)(2,1)}, u32[]{:S(2)}, u32[]{:S(2)}) collective-permute-start(bf16[4,128,512]{2,1,0:T(8,128)(2,1)} %get-tuple-element.80), channel_id=1, source_target_pairs={{0,1},{1,2},{2,3},{3,4},{4,5},{5,6},{6,7},{8,9},{9,10},{10,11},{11... | collective-permute-start | bytes 1572872 | tf_op jit(solution)/shard_map/ppermute | solution.py:495
  133.6 19.5 %collective-permute-start.12 = (bf16[4,128,256]{2,1,0:T(8,128)(2,1)}, bf16[4,128,256]{2,1,0:T(8,128)(2,1)}, u32[]{:S(2)}, u32[]{:S(2)}) collective-permute-start(bf16[4,128,256]{2,1,0:T(8,128)(2,1)} %get-tuple-element.99), channel_id=1, source_target_pairs={{0,1},{1,2},{2,3},{3,4},{4,5},{5,6},{6,7},{8,9},{9,10},{10,11},{11... | collective-permute-start | bytes 786440 | tf_op jit(solution)/shard_map/ppermute | solution.py:495

commit v2 on v1

--- a/solution.py
+++ b/solution.py
@@ -510,7 +510,7 @@
     halo_g0 = send(dg1, "outer_right")
     halo_g1 = send(dg0, "outer_left")
     ready = (halo_out, ks, halo_g0, halo_g1)
-    from_right = [send(after(x, *ready), "left") for x in col0]
+    from_right = [send(after(x, *(ready if n else ready[:2])), "left") for n, x in enumerate(col0)]
     pos = after(pos, delta0)
 
     *parts, dqp = local(pos, q, do, k, v, ks, lse, (delta0, delta1), (used0, used1))

time: 157 us -> 163 us (1.038)
  waiting for transfers between devices: 9.99 us -> 15.1 us
    ppermute x14, waiting for transfers between devices: 9.99 us -> 15.1 us  [on_device(): send = lambda x, way: lax.ppermute(x, AXES, pairs[way])]
  transfers between devices with their start and end apart: 14 -> 14, of which waited for: 4 -> 4; matrix products, arithmetic and copies ran while one was open for 1% -> 1% of each run, Pallas kernels for 54% -> 53%
where the time goes in v2:
time: 163 us; the launch traced here: 161 us
  Pallas kernels  87.2 us (53%)
  starting transfers between devices  54.3 us (33%)
  waiting for transfers between devices  15.1 us (9%)
  local copies, waits for them, and re-layouts  1.81 us (1%)
    ppermute x14, starting transfers between devices, on_device(): send = lambda x, way: lax.ppermute(x, AXES, pairs[way])  54.3 us
    pallas_call x1, Pallas kernels, local(): call(local_kernel, 'local', PAIRS, [lanes_spec(TILES)] * 4 + [lanes_spec(...  28.3 us
    pallas_call x3, Pallas kernels, column(): call(functools.partial(column_kernel, side=side, sub=sub), 'column', coun...  25.8 us
    ppermute x14, waiting for transfers between devices, on_device(): send = lambda x, way: lax.ppermute(x, AXES, pairs[way])  15.1 us
    pallas_call x2, Pallas kernels, prepare_column(): call(functools.partial(prepare_column_kernel, c=c), 'prepare_column', 4,...  9.83 us
    pallas_call x3, Pallas kernels, finish_queries(): call(queries_kernel, 'finish_queries', 2, [block, rows_spec((2, BLK, wide...  8.88 us
    pallas_call x1, Pallas kernels, outers(): call(outer_kernel, 'outer_rows', PAIRS // SUB, [outer] * 2 + [lanes_spec(...  6.62 us
    pallas_call x1, Pallas kernels, finish_edges(): call(edges_kernel, 'finish_edges', 2, [rows_spec((1,) + edge)] + [fixed(e...  4.3 us
  transfers between devices with their start and end apart: 14, of which 4 were waited for; matrix products, arithmetic and copies ran while one was open for 1% of the time, Pallas kernels for 53%

profile of v2, /device:TPU:96, one launch (start us, length us, event | category | flops | bytes accessed | tf_op | source)
XLA Modules:
  0.0 160.7 jit_solution(18188248096111260167)
XLA Ops:
  0.6 0.0 copy-start
  0.7 1.2 constant_dynamic-slice_fusion
  1.8 0.9 pad_maximum_fusion
  2.8 0.0 collective-permute-start
  2.8 0.0 copy-done
  2.8 0.6 copy.23.lse_ref
  3.4 0.6 pad_add_fusion.pos_ref
  4.0 3.4 %prepare_row.1 = (bf16[2,272,768]{2,1,0:T(8,128)(2,1)}, bf16[1,272,768]{2,1,0:T(8,128)(2,1)}, bf16[1,272,768]{2,1,0:T(8,128)(2,1)}) custom-call(s32[3]{0:T(128)} %pad_add_fusion.pos_ref, s32[4,2,8]{2,1,0:T(2,128)} %near_ref.5, s32[4,2,8]{2,1,0:T(2,128)} %flag_ref.5, bf16[4,2,128,768]{3,2,1,0:T(8,128)(2,1)} %q_ref.7, bf16[4,2,128,768]{3,2,1,0:T(8,128)(2,1)} %do_ref.7, ...), custom_call_target="tpu_custom_call" | custom-call | flops 1 | bytes 1 | tf_op jit(solution)/shard_map/prepare_row/pallas_call | solution.py:373
  7.4 5.5 %collective-permute-start.1 = (bf16[2,272,768]{2,1,0:T(8,128)(2,1)}, bf16[2,272,768]{2,1,0:T(8,128)(2,1)}, u32[]{:S(2)}, u32[]{:S(2)}) collective-permute-start(bf16[2,272,768]{2,1,0:T(8,128)(2,1)} %get-tuple-element.52), channel_id=1, source_target_pairs={{0,120},{1,121},{2,122},{3,123},{4,124},{5,125},{6,126},{7,127},{8... | collective-permute-start | bytes 2506760 | tf_op jit(solution)/shard_map/ppermute | solution.py:495
  12.9 4.9 %prepare_column.2 = (f32[4,12,128]{2,1,0:T(8,128)}, f32[4,16,128]{2,1,0:T(8,128)}, bf16[4,272,768]{2,1,0:T(8,128)(2,1)}) custom-call(s32[3]{0:T(128)} %pad_add_fusion.pos_ref, s32[4,2,8]{2,1,0:T(2,128)} %near_ref.5, s32[4,2,8]{2,1,0:T(2,128)} %flag_ref.5, bf16[4,2,128,768]{3,2,1,0:T(8,128)(2,1)} %q_ref.7, bf16[4,2,128,768]{3,2,1,0:T(8,128)(2,1)} %do_ref.7, ...), custom_call_target="tpu_custom_call" | custom-call | flops 1 | bytes 1 | tf_op jit(solution)/shard_map/prepare_column/pallas_call | solution.py:359
  17.9 0.0 collective-permute-done.ks_ref
  17.9 2.6 %collective-permute-start.4 = (bf16[4,272,768]{2,1,0:T(8,128)(2,1)}, bf16[4,272,768]{2,1,0:T(8,128)(2,1)}, u32[]{:S(2)}, u32[]{:S(2)}) collective-permute-start(bf16[4,272,768]{2,1,0:T(8,128)(2,1)} %get-tuple-element.67), channel_id=1, source_target_pairs={{0,1},{1,2},{2,3},{3,4},{4,5},{5,6},{6,7},{8,9},{9,10},{10,11},{11... | collective-permute-start | bytes 5013512 | tf_op jit(solution)/shard_map/ppermute | solution.py:495
  20.5 4.9 %prepare_column.3 = (f32[4,12,128]{2,1,0:T(8,128)}, f32[4,16,128]{2,1,0:T(8,128)}, bf16[4,272,512]{2,1,0:T(8,128)(2,1)}, bf16[4,272,256]{2,1,0:T(8,128)(2,1)}) custom-call(s32[3]{0:T(128)} %pad_add_fusion.pos_ref, s32[4,2,8]{2,1,0:T(2,128)} %near_ref.5, s32[4,2,8]{2,1,0:T(2,128)} %flag_ref.5, bf16[4,2,128,768]{3,2,1,0:T(8,128)(2,1)} %q_ref.7, ...), custom_call_target="tpu_custom_call" | custom-call | flops 1 | bytes 1 | tf_op jit(solution)/shard_map/prepare_column/pallas_call | solution.py:359
  25.4 0.0 collective-permute-done.1.out_ref
  25.4 4.2 %collective-permute-start.5 = (bf16[4,272,512]{2,1,0:T(8,128)(2,1)}, bf16[4,272,512]{2,1,0:T(8,128)(2,1)}, u32[]{:S(2)}, u32[]{:S(2)}) collective-permute-start(bf16[4,272,512]{2,1,0:T(8,128)(2,1)} %get-tuple-element.75), channel_id=1, source_target_pairs={{1,0},{2,1},{3,2},{4,3},{5,4},{6,5},{7,6},{9,8},{10,9},{11,10},{12... | collective-permute-start | bytes 3342344 | tf_op jit(solution)/shard_map/ppermute | solution.py:495
  29.5 4.4 %collective-permute-start.2 = (bf16[1,272,768]{2,1,0:T(8,128)(2,1)}, bf16[1,272,768]{2,1,0:T(8,128)(2,1)}, u32[]{:S(2)}, u32[]{:S(2)}) collective-permute-start(bf16[1,272,768]{2,1,0:T(8,128)(2,1)} %get-tuple-element.62), channel_id=1, source_target_pairs={{0,121},{1,122},{2,123},{3,124},{4,125},{5,126},{6,127},{8,17},{9,... | collective-permute-start | bytes 1253384 | tf_op jit(solution)/shard_map/ppermute | solution.py:495
  34.0 5.3 %collective-permute-start.3 = (bf16[1,272,768]{2,1,0:T(8,128)(2,1)}, bf16[1,272,768]{2,1,0:T(8,128)(2,1)}, u32[]{:S(2)}, u32[]{:S(2)}) collective-permute-start(bf16[1,272,768]{2,1,0:T(8,128)(2,1)} %get-tuple-element.63), channel_id=1, source_target_pairs={{1,120},{2,121},{3,122},{4,123},{5,124},{6,125},{7,126},{9,16},{10... | collective-permute-start | bytes 1253384 | tf_op jit(solution)/shard_map/ppermute | solution.py:495
  39.3 6.9 %collective-permute-done.2.dg0_ref = bf16[1,272,768]{2,1,0:T(8,128)(2,1)} collective-permute-done((bf16[1,272,768]{2,1,0:T(8,128)(2,1)}, bf16[1,272,768]{2,1,0:T(8,128)(2,1)}, u32[]{:S(2)}, u32[]{:S(2)}) %collective-permute-start.2) | collective-permute-done | bytes 417824 | tf_op jit(solution)/shard_map/ppermute | solution.py:495
  46.3 0.7 collective-permute-done.3.dg1_ref
  47.0 2.4 %collective-permute-start.10 = (bf16[4,272,256]{2,1,0:T(8,128)(2,1)}, bf16[4,272,256]{2,1,0:T(8,128)(2,1)}, u32[]{:S(2)}, u32[]{:S(2)}) collective-permute-start(bf16[4,272,256]{2,1,0:T(8,128)(2,1)} %get-tuple-element.86), channel_id=1, source_target_pairs={{1,0},{2,1},{3,2},{4,3},{5,4},{6,5},{7,6},{9,8},{10,9},{11,10},{12... | collective-permute-start | bytes 1671176 | tf_op jit(solution)/shard_map/ppermute | solution.py:495
  49.4 28.3 %local.1 = (f32[4,2,128,768]{3,2,1,0:T(8,128)}, f32[4,2,128,768]{3,2,1,0:T(8,128)}, f32[2,128,768]{2,1,0:T(8,128)}, f32[2,128,768]{2,1,0:T(8,128)}, f32[4,2,128,768]{3,2,1,0:T(8,128)}) custom-call(s32[3]{0:T(128)} %pad_add_fusion.pos_ref, bf16[4,2,128,768]{3,2,1,0:T(8,128)(2,1)} %q_ref.7, bf16[4,2,128,768]{3,2,1,0:T(8,128)(2,1)} %do_ref.7, ...), custom_call_target="tpu_custom_call" | custom-call | flops 1 | bytes 1 | tf_op jit(solution)/shard_map/local/pallas_call | solution.py:387
  77.7 6.6 %outer_rows.1 = (f32[2,2,128,768]{3,2,1,0:T(8,128)}, bf16[2,128,768]{2,1,0:T(8,128)(2,1)}, bf16[1,128,768]{2,1,0:T(8,128)(2,1)}, bf16[1,128,768]{2,1,0:T(8,128)(2,1)}) custom-call(s32[3]{0:T(128)} %pad_add_fusion.pos_ref, bf16[4,2,128,768]{3,2,1,0:T(8,128)(2,1)} %k_ref.9, bf16[4,2,128,768]{3,2,1,0:T(8,128)(2,1)} %v_ref.9, ...), custom_call_target="tpu_custom_call" | custom-call | flops 1 | bytes 1 | tf_op jit(solution)/shard_map/outer_rows/pallas_call | solution.py:434
  84.3 5.2 %collective-permute-start.6 = (bf16[2,128,768]{2,1,0:T(8,128)(2,1)}, bf16[2,128,768]{2,1,0:T(8,128)(2,1)}, u32[]{:S(2)}, u32[]{:S(2)}) collective-permute-start(bf16[2,128,768]{2,1,0:T(8,128)(2,1)} %get-tuple-element.64), channel_id=1, source_target_pairs={{0,120},{1,121},{2,122},{3,123},{4,124},{5,125},{6,126},{7,127},{8... | collective-permute-start | bytes 1179656 | tf_op jit(solution)/shard_map/ppermute | solution.py:495
  89.5 0.0 collective-permute-done.4.col_ref
  89.5 11.2 %column.3 = (bf16[4,2,128,768]{3,2,1,0:T(8,128)(2,1)}, bf16[4,2,128,768]{3,2,1,0:T(8,128)(2,1)}, bf16[2,2,128,768]{3,2,1,0:T(8,128)(2,1)}, f32[2,2,2,128,768]{4,3,2,1,0:T(8,128)}, bf16[4,128,768]{2,1,0:T(8,128)(2,1)}) custom-call(s32[3]{0:T(128)} %pad_add_fusion.pos_ref, bf16[4,2,128,768]{3,2,1,0:T(8,128)(2,1)} %k_ref.9, bf16[4,2,128,768]{3,2,1,0:T(8,128)(2,1)} %v_ref.9, ...), custom_call_target="tpu_custom_call" | custom-call | flops 1 | bytes 1 | tf_op jit(solution)/shard_map/column/pallas_call | solution.py:406
  100.7 1.9 %collective-permute-start.9 = (bf16[4,128,768]{2,1,0:T(8,128)(2,1)}, bf16[4,128,768]{2,1,0:T(8,128)(2,1)}, u32[]{:S(2)}, u32[]{:S(2)}) collective-permute-start(bf16[4,128,768]{2,1,0:T(8,128)(2,1)} %get-tuple-element.72), channel_id=1, source_target_pairs={{1,0},{2,1},{3,2},{4,3},{5,4},{6,5},{7,6},{9,8},{10,9},{11,10},{12... | collective-permute-start | bytes 2359304 | tf_op jit(solution)/shard_map/ppermute | solution.py:495
  102.6 4.1 %collective-permute-start.7 = (bf16[1,128,768]{2,1,0:T(8,128)(2,1)}, bf16[1,128,768]{2,1,0:T(8,128)(2,1)}, u32[]{:S(2)}, u32[]{:S(2)}) collective-permute-start(bf16[1,128,768]{2,1,0:T(8,128)(2,1)} %get-tuple-element.81), channel_id=1, source_target_pairs={{0,121},{1,122},{2,123},{3,124},{4,125},{5,126},{6,127},{8,17},{9,... | collective-permute-start | bytes 589832 | tf_op jit(solution)/shard_map/ppermute | solution.py:495
  106.7 0.0 collective-permute-done.5.col_ref
  106.7 5.7 %collective-permute-start.8 = (bf16[1,128,768]{2,1,0:T(8,128)(2,1)}, bf16[1,128,768]{2,1,0:T(8,128)(2,1)}, u32[]{:S(2)}, u32[]{:S(2)}) collective-permute-start(bf16[1,128,768]{2,1,0:T(8,128)(2,1)} %get-tuple-element.82), channel_id=1, source_target_pairs={{1,120},{2,121},{3,122},{4,123},{5,124},{6,125},{7,126},{9,16},{10... | collective-permute-start | bytes 589832 | tf_op jit(solution)/shard_map/ppermute | solution.py:495
  112.4 8.5 %column.4 = (bf16[4,2,128,768]{3,2,1,0:T(8,128)(2,1)}, bf16[4,2,128,768]{3,2,1,0:T(8,128)(2,1)}, bf16[2,2,128,768]{3,2,1,0:T(8,128)(2,1)}, f32[2,2,2,128,768]{4,3,2,1,0:T(8,128)}, bf16[4,128,512]{2,1,0:T(8,128)(2,1)}) custom-call(s32[3]{0:T(128)} %pad_add_fusion.pos_ref, ...), custom_call_target="tpu_custom_call", output_to_operand_aliasing={{0}: (9, {}), {1}: (10, {}), {2}: (11, {}), {3}: (12, {})} | custom-call | flops 1 | bytes 1 | tf_op jit(solution)/shard_map/column/pallas_call | solution.py:406
  120.9 0.0 collective-permute-done.7.corner_ref
  120.9 0.0 collective-permute-done.8.corner_ref
  120.9 0.0 collective-permute-done.6.row_ref
  120.9 0.0 collective-permute-done.10.col_ref
  121.0 6.1 %column.5 = (bf16[4,2,128,768]{3,2,1,0:T(8,128)(2,1)}, bf16[4,2,128,768]{3,2,1,0:T(8,128)(2,1)}, bf16[2,2,128,768]{3,2,1,0:T(8,128)(2,1)}, f32[2,2,2,128,768]{4,3,2,1,0:T(8,128)}, bf16[4,128,256]{2,1,0:T(8,128)(2,1)}) custom-call(s32[3]{0:T(128)} %pad_add_fusion.pos_ref, ...), custom_call_target="tpu_custom_call", output_to_operand_aliasing={{0}: (9, {}), {1}: (10, {}), {2}: (11, {}), {3}: (12, {})} | custom-call | flops 1 | bytes 1 | tf_op jit(solution)/shard_map/column/pallas_call | solution.py:406
  127.1 8.5 %collective-permute-start.11 = (bf16[2,2,128,768]{3,2,1,0:T(8,128)(2,1)}, bf16[2,2,128,768]{3,2,1,0:T(8,128)(2,1)}, u32[]{:S(2)}, u32[]{:S(2)}) collective-permute-start(bf16[2,2,128,768]{3,2,1,0:T(8,128)(2,1)} %get-tuple-element.93), channel_id=1, source_target_pairs={{0,8},{1,9},{2,10},{3,11},{4,12},{5,13},{6,14},{7,15},{8,0},{9,1},... | collective-permute-start | bytes 2359304 | tf_op jit(solution)/shard_map/ppermute | solution.py:495
  135.6 2.6 %collective-permute-start.13 = (bf16[4,128,512]{2,1,0:T(8,128)(2,1)}, bf16[4,128,512]{2,1,0:T(8,128)(2,1)}, u32[]{:S(2)}, u32[]{:S(2)}) collective-permute-start(bf16[4,128,512]{2,1,0:T(8,128)(2,1)} %get-tuple-element.80), channel_id=1, source_target_pairs={{0,1},{1,2},{2,3},{3,4},{4,5},{5,6},{6,7},{8,9},{9,10},{10,11},{11... | collective-permute-start | bytes 1572872 | tf_op jit(solution)/shard_map/ppermute | solution.py:495
  138.2 0.0 collective-permute-done.9.back_ref
  138.2 1.9 %collective-permute-start.12 = (bf16[4,128,256]{2,1,0:T(8,128)(2,1)}, bf16[4,128,256]{2,1,0:T(8,128)(2,1)}, u32[]{:S(2)}, u32[]{:S(2)}) collective-permute-start(bf16[4,128,256]{2,1,0:T(8,128)(2,1)} %get-tuple-element.99), channel_id=1, source_target_pairs={{0,1},{1,2},{2,3},{3,4},{4,5},{5,6},{6,7},{8,9},{9,10},{10,11},{11... | collective-permute-start | bytes 786440 | tf_op jit(solution)/shard_map/ppermute | solution.py:495
  140.1 3.3 %finish_queries.3.rest_0_ = bf16[4,2,128,768]{3,2,1,0:T(8,128)(2,1)} custom-call(s32[3]{0:T(128)} %pad_add_fusion.pos_ref, f32[4,2,128,768]{3,2,1,0:T(8,128)} %get-tuple-element.60.dq_ref, bf16[4,128,768]{2,1,0:T(8,128)(2,1)} %collective-permute-done.9.back_ref, bf16[2,128,768]{2,1,0:T(8,128)(2,1)} %collective-permute-done.6.row_ref, ...), custom_call_target="tpu_custom_call" | custom-call | flops 1 | bytes 1 | tf_op jit(solution)/shard_map/finish_queries/pallas_call | solution.py:449
  143.5 0.0 collective-permute-done.11.sib_ref
  143.5 4.3 %finish_edges.1 = (bf16[4,2,128,768]{3,2,1,0:T(8,128)(2,1)}, bf16[4,2,128,768]{3,2,1,0:T(8,128)(2,1)}) custom-call(s32[3]{0:T(128)} %pad_add_fusion.pos_ref, f32[2,2,2,128,768]{4,3,2,1,0:T(8,128)} %get-tuple-element.91.tail_ref, f32[2,2,128,768]{3,2,1,0:T(8,128)} %get-tuple-element.92.part_ref, ...), custom_call_target="tpu_custom_call", output_to_operand_aliasing={{0}: (4, {}), {1}: (5, {})} | custom-call | flops 1 | bytes 1 | tf_op jit(solution)/shard_map/finish_edges/pallas_call | solution.py:463
  147.8 5.7 %collective-permute-done.13.back_ref = bf16[4,128,512]{2,1,0:T(8,128)(2,1)} collective-permute-done((bf16[4,128,512]{2,1,0:T(8,128)(2,1)}, bf16[4,128,512]{2,1,0:T(8,128)(2,1)}, u32[]{:S(2)}, u32[]{:S(2)}) %collective-permute-start.13) | collective-permute-done | bytes 524320 | tf_op jit(solution)/shard_map/ppermute | solution.py:495
  153.4 2.9 %finish_queries.4.rest_0_ = bf16[4,2,128,768]{3,2,1,0:T(8,128)(2,1)} custom-call(s32[3]{0:T(128)} %pad_add_fusion.pos_ref, f32[4,2,128,768]{3,2,1,0:T(8,128)} %get-tuple-element.60.dq_ref, bf16[4,128,512]{2,1,0:T(8,128)(2,1)} %collective-permute-done.13.back_ref, ...), custom_call_target="tpu_custom_call", output_to_operand_aliasing={{}: (5, {})} | custom-call | flops 1 | bytes 1 | tf_op jit(solution)/shard_map/finish_queries/pallas_call | solution.py:449
  156.4 1.7 %collective-permute-done.12.back_ref = bf16[4,128,256]{2,1,0:T(8,128)(2,1)} collective-permute-done((bf16[4,128,256]{2,1,0:T(8,128)(2,1)}, bf16[4,128,256]{2,1,0:T(8,128)(2,1)}, u32[]{:S(2)}, u32[]{:S(2)}) %collective-permute-start.12) | collective-permute-done | bytes 262176 | tf_op jit(solution)/shard_map/ppermute | solution.py:495
  158.1 2.6 %finish_queries.5 = bf16[4,2,128,768]{3,2,1,0:T(8,128)(2,1)} custom-call(s32[3]{0:T(128)} %pad_add_fusion.pos_ref, f32[4,2,128,768]{3,2,1,0:T(8,128)} %get-tuple-element.60.dq_ref, bf16[4,128,256]{2,1,0:T(8,128)(2,1)} %collective-permute-done.12.back_ref, bf16[2,128,768]{2,1,0:T(8,128)(2,1)} %collective-permute-done.6.row_ref, ...), custom_call_target="tpu_custom_call", output_to_operand_aliasing={{}: (5, {})} | custom-call | flops 1 | bytes 1 | tf_op jit(solution)/shard_map/finish_queries/pallas_call | solution.py:449
Async XLA Ops:
  0.6 2.1 %copy-start = (f32[4,2,12,128]{3,1,2,0:T(2,128)S(1)}, f32[4,2,12,128]{3,1,2,0:T(2,128)}, u32[]{:S(2)}) copy-start(f32[4,2,12,128]{3,1,2,0:T(2,128)} %param.13) | copy-start | bytes 147460
  2.8 15.1 %collective-permute-start = (bf16[2,2,128,768]{3,2,1,0:T(8,128)(2,1)}, bf16[2,2,128,768]{3,2,1,0:T(8,128)(2,1)}, u32[]{:S(2)}, u32[]{:S(2)}) collective-permute-start(bf16[2,2,128,768]{3,2,1,0:T(8,128)(2,1)} %pad_maximum_fusion), channel_id=1, source_target_pairs={{0,8},{1,9},{2,10},{3,11},{4,12},{5,13},{6,14},{7,15},{8,0},{9,1},... | collective-permute-start | bytes 2359304 | tf_op jit(solution)/shard_map/ppermute | solution.py:495
  7.4 17.9 %collective-permute-start.1 = (bf16[2,272,768]{2,1,0:T(8,128)(2,1)}, bf16[2,272,768]{2,1,0:T(8,128)(2,1)}, u32[]{:S(2)}, u32[]{:S(2)}) collective-permute-start(bf16[2,272,768]{2,1,0:T(8,128)(2,1)} %get-tuple-element.52), channel_id=1, source_target_pairs={{0,120},{1,121},{2,122},{3,123},{4,124},{5,125},{6,126},{7,127},{8... | collective-permute-start | bytes 2506760 | tf_op jit(solution)/shard_map/ppermute | solution.py:495
  17.9 71.6 %collective-permute-start.4 = (bf16[4,272,768]{2,1,0:T(8,128)(2,1)}, bf16[4,272,768]{2,1,0:T(8,128)(2,1)}, u32[]{:S(2)}, u32[]{:S(2)}) collective-permute-start(bf16[4,272,768]{2,1,0:T(8,128)(2,1)} %get-tuple-element.67), channel_id=1, source_target_pairs={{0,1},{1,2},{2,3},{3,4},{4,5},{5,6},{6,7},{8,9},{9,10},{10,11},{11... | collective-permute-start | bytes 5013512 | tf_op jit(solution)/shard_map/ppermute | solution.py:495
  25.4 81.3 %collective-permute-start.5 = (bf16[4,272,512]{2,1,0:T(8,128)(2,1)}, bf16[4,272,512]{2,1,0:T(8,128)(2,1)}, u32[]{:S(2)}, u32[]{:S(2)}) collective-permute-start(bf16[4,272,512]{2,1,0:T(8,128)(2,1)} %get-tuple-element.75), channel_id=1, source_target_pairs={{1,0},{2,1},{3,2},{4,3},{5,4},{6,5},{7,6},{9,8},{10,9},{11,10},{12... | collective-permute-start | bytes 3342344 | tf_op jit(solution)/shard_map/ppermute | solution.py:495
  29.5 16.7 %collective-permute-start.2 = (bf16[1,272,768]{2,1,0:T(8,128)(2,1)}, bf16[1,272,768]{2,1,0:T(8,128)(2,1)}, u32[]{:S(2)}, u32[]{:S(2)}) collective-permute-start(bf16[1,272,768]{2,1,0:T(8,128)(2,1)} %get-tuple-element.62), channel_id=1, source_target_pairs={{0,121},{1,122},{2,123},{3,124},{4,125},{5,126},{6,127},{8,17},{9,... | collective-permute-start | bytes 1253384 | tf_op jit(solution)/shard_map/ppermute | solution.py:495
  34.0 13.0 %collective-permute-start.3 = (bf16[1,272,768]{2,1,0:T(8,128)(2,1)}, bf16[1,272,768]{2,1,0:T(8,128)(2,1)}, u32[]{:S(2)}, u32[]{:S(2)}) collective-permute-start(bf16[1,272,768]{2,1,0:T(8,128)(2,1)} %get-tuple-element.63), channel_id=1, source_target_pairs={{1,120},{2,121},{3,122},{4,123},{5,124},{6,125},{7,126},{9,16},{10... | collective-permute-start | bytes 1253384 | tf_op jit(solution)/shard_map/ppermute | solution.py:495
  47.0 73.9 %collective-permute-start.10 = (bf16[4,272,256]{2,1,0:T(8,128)(2,1)}, bf16[4,272,256]{2,1,0:T(8,128)(2,1)}, u32[]{:S(2)}, u32[]{:S(2)}) collective-permute-start(bf16[4,272,256]{2,1,0:T(8,128)(2,1)} %get-tuple-element.86), channel_id=1, source_target_pairs={{1,0},{2,1},{3,2},{4,3},{5,4},{6,5},{7,6},{9,8},{10,9},{11,10},{12... | collective-permute-start | bytes 1671176 | tf_op jit(solution)/shard_map/ppermute | solution.py:495
  84.3 36.6 %collective-permute-start.6 = (bf16[2,128,768]{2,1,0:T(8,128)(2,1)}, bf16[2,128,768]{2,1,0:T(8,128)(2,1)}, u32[]{:S(2)}, u32[]{:S(2)}) collective-permute-start(bf16[2,128,768]{2,1,0:T(8,128)(2,1)} %get-tuple-element.64), channel_id=1, source_target_pairs={{0,120},{1,121},{2,122},{3,123},{4,124},{5,125},{6,126},{7,127},{8... | collective-permute-start | bytes 1179656 | tf_op jit(solution)/shard_map/ppermute | solution.py:495
  100.7 37.5 %collective-permute-start.9 = (bf16[4,128,768]{2,1,0:T(8,128)(2,1)}, bf16[4,128,768]{2,1,0:T(8,128)(2,1)}, u32[]{:S(2)}, u32[]{:S(2)}) collective-permute-start(bf16[4,128,768]{2,1,0:T(8,128)(2,1)} %get-tuple-element.72), channel_id=1, source_target_pairs={{1,0},{2,1},{3,2},{4,3},{5,4},{6,5},{7,6},{9,8},{10,9},{11,10},{12... | collective-permute-start | bytes 2359304 | tf_op jit(solution)/shard_map/ppermute | solution.py:495
  102.6 18.3 %collective-permute-start.7 = (bf16[1,128,768]{2,1,0:T(8,128)(2,1)}, bf16[1,128,768]{2,1,0:T(8,128)(2,1)}, u32[]{:S(2)}, u32[]{:S(2)}) collective-permute-start(bf16[1,128,768]{2,1,0:T(8,128)(2,1)} %get-tuple-element.81), channel_id=1, source_target_pairs={{0,121},{1,122},{2,123},{3,124},{4,125},{5,126},{6,127},{8,17},{9,... | collective-permute-start | bytes 589832 | tf_op jit(solution)/shard_map/ppermute | solution.py:495
  106.7 14.2 %collective-permute-start.8 = (bf16[1,128,768]{2,1,0:T(8,128)(2,1)}, bf16[1,128,768]{2,1,0:T(8,128)(2,1)}, u32[]{:S(2)}, u32[]{:S(2)}) collective-permute-start(bf16[1,128,768]{2,1,0:T(8,128)(2,1)} %get-tuple-element.82), channel_id=1, source_target_pairs={{1,120},{2,121},{3,122},{4,123},{5,124},{6,125},{7,126},{9,16},{10... | collective-permute-start | bytes 589832 | tf_op jit(solution)/shard_map/ppermute | solution.py:495
  127.1 16.4 %collective-permute-start.11 = (bf16[2,2,128,768]{3,2,1,0:T(8,128)(2,1)}, bf16[2,2,128,768]{3,2,1,0:T(8,128)(2,1)}, u32[]{:S(2)}, u32[]{:S(2)}) collective-permute-start(bf16[2,2,128,768]{3,2,1,0:T(8,128)(2,1)} %get-tuple-element.93), channel_id=1, source_target_pairs={{0,8},{1,9},{2,10},{3,11},{4,12},{5,13},{6,14},{7,15},{8,0},{9,1},... | collective-permute-start | bytes 2359304 | tf_op jit(solution)/shard_map/ppermute | solution.py:495
  135.6 17.9 %collective-permute-start.13 = (bf16[4,128,512]{2,1,0:T(8,128)(2,1)}, bf16[4,128,512]{2,1,0:T(8,128)(2,1)}, u32[]{:S(2)}, u32[]{:S(2)}) collective-permute-start(bf16[4,128,512]{2,1,0:T(8,128)(2,1)} %get-tuple-element.80), channel_id=1, source_target_pairs={{0,1},{1,2},{2,3},{3,4},{4,5},{5,6},{6,7},{8,9},{9,10},{10,11},{11... | collective-permute-start | bytes 1572872 | tf_op jit(solution)/shard_map/ppermute | solution.py:495
  138.2 19.9 %collective-permute-start.12 = (bf16[4,128,256]{2,1,0:T(8,128)(2,1)}, bf16[4,128,256]{2,1,0:T(8,128)(2,1)}, u32[]{:S(2)}, u32[]{:S(2)}) collective-permute-start(bf16[4,128,256]{2,1,0:T(8,128)(2,1)} %get-tuple-element.99), channel_id=1, source_target_pairs={{0,1},{1,2},{2,3},{3,4},{4,5},{5,6},{6,7},{8,9},{9,10},{10,11},{11... | collective-permute-start | bytes 786440 | tf_op jit(solution)/shard_map/ppermute | solution.py:495
